TPU v7x, 32 devices: a whole 2x2x4 slice. The times are simulated.
32 devices in a mesh: dp: 2 (over y), expert: 16 (over z, x, core).
Axes of the slice: x: 2, y: 2, z: 4, core: 2. Of those that a mesh axis runs over, the one named last changes fastest.
Arguments:
- cache: bfloat16 [4, 64, 1152], P('dp'), may hold values from -6 to 6
- requests: int32 [2, 16, 2], P(None, 'expert'), may hold values from 0 to 3
- routes: int32 [4096, 1], P('expert'), may hold values from 0 to 15; in each aligned block of 256 rows (0 to 255, 256 to 511, ...) at most 20 rows name the same one
- combine_weight: float32 [4096, 1], P('expert'), may hold values from 0.2 to 1
- proj_weight: bfloat16 [1152, 2048], P('expert', 'dp'), may hold values from -1 to 1
- norm_gain: float32 [2048], replicated, may hold values from 0.5 to 1.5
- gate_weight: bfloat16 [16, 2048, 1408], P('expert', None, 'dp'), may hold values from -0.125 to 0.125
- up_weight: bfloat16 [16, 2048, 1408], P('expert', None, 'dp'), may hold values from -0.125 to 0.125
- down_weight: bfloat16 [16, 1408, 2048], P('expert', None, 'dp'), may hold values from -0.15625 to 0.15625
- cotangent: bfloat16 [4096, 2048], P('expert', 'dp'), may hold values from -6 to 6
Outputs:
- mixed: bfloat16 [4096, 2048], P('expert', 'dp')
- down_grad: bfloat16 [16, 1408, 2048], P('expert', None, 'dp')
Inputs may be any that keep to these rules, and one draw needn't show every extreme that they name: `routes`: among the 256 tokens of one column no expert is named more than 20 times, and in every draw some column names some expert exactly 20 times.
All inputs are finite; a program needn't handle non-finite values.
Results may differ from a plain program's by a relative error of at most 0.012.
Values may be sent and summed in bfloat16 or wider, within the bound.
A program may use at most 64 MiB of HBM per device.

v0:
```python
import jax
import jax.numpy as jnp
from jax import lax
from jax.sharding import PartitionSpec as P


def normalize(row_block, gain_row, sum_squares, model_width):
    inv_scale = lax.rsqrt(sum_squares / model_width + 1e-06)
    return (row_block.astype(jnp.float32) * inv_scale[:, None] * gain_row[None, :]).astype(
        jnp.bfloat16
    )


def local_squares(row_block):
    values = row_block.astype(jnp.float32)
    return jnp.sum(values * values, axis=1)


def body(
    cache,
    requests,
    routes,
    combine_weight,
    proj_weight,
    norm_gain,
    gate_weight,
    up_weight,
    down_weight,
    cotangent,
):
    dp_rank = lax.axis_index("dp")
    model_width = norm_gain.shape[0]
    slice_width = cotangent.shape[1]
    wanted = requests.reshape(-1)
    request_count = wanted.shape[0]
    shard_piece = lax.all_gather(cache, "dp", axis=0, tiled=True)
    matches = (wanted[:, None] == jnp.arange(shard_piece.shape[0])[None, :]).astype(jnp.bfloat16)
    matched = jnp.einsum("rk,kpf->rpf", matches, shard_piece, preferred_element_type=jnp.float32)
    fetched = matched.astype(jnp.bfloat16)
    features = fetched.reshape(request_count * cache.shape[1], cache.shape[2])
    tokens = features.shape[0]
    projected = jnp.dot(
        features,
        lax.all_gather(proj_weight, "expert", axis=0, tiled=True),
        preferred_element_type=jnp.float32,
    ).astype(jnp.bfloat16)
    gain_slice = lax.dynamic_slice_in_dim(norm_gain, dp_rank * slice_width, slice_width)
    sum_squares = lax.psum(local_squares(projected), "dp")
    source_rows = normalize(projected, gain_slice, sum_squares, model_width)
    experts = lax.axis_size("expert") * gate_weight.shape[0]
    capacity = max(2, 5 * tokens // (4 * experts))
    expert_id = routes[:, 0]
    onehot = (expert_id[:, None] == jnp.arange(experts, dtype=jnp.int32)[None, :]).astype(jnp.int32)
    slot_rank = jnp.sum((jnp.cumsum(onehot, axis=0) - 1) * onehot, axis=1)
    position = expert_id * capacity + slot_rank
    slot_map = (
        jnp.zeros((experts * capacity,), jnp.int32)
        .at[position]
        .set(jnp.arange(tokens, dtype=jnp.int32) + 1)
    )
    filled = slot_map > 0
    source_row = jnp.maximum(slot_map - 1, 0)

    def arrange(row_block):
        picked = jnp.where(filled[:, None], row_block[source_row], jnp.zeros((), row_block.dtype))
        return picked.reshape(experts, capacity, row_block.shape[1])

    token_weight = combine_weight[:, 0]
    scaled_grad = (token_weight[:, None] * cotangent.astype(jnp.float32)).astype(jnp.bfloat16)
    sent_rows, sent_grad = (
        lax.all_to_all(arrange(source_rows), "expert", split_axis=0, concat_axis=0, tiled=True),
        lax.all_to_all(arrange(scaled_grad), "expert", split_axis=0, concat_axis=0, tiled=True),
    )
    slot_count = sent_rows.shape[0] * sent_rows.shape[1]
    full_rows = lax.all_gather(sent_rows.reshape(slot_count, slice_width), "dp", axis=1, tiled=True)
    grad_rows = sent_grad.reshape(slot_count, slice_width)
    gate_act = jnp.dot(full_rows, gate_weight[0], preferred_element_type=jnp.float32)
    up_act = jnp.dot(full_rows, up_weight[0], preferred_element_type=jnp.float32)
    hidden = (jax.nn.silu(gate_act) * up_act).astype(jnp.bfloat16)
    down_local = down_weight[0]
    shard_piece = lax.all_gather(hidden, "dp", axis=1, tiled=True)
    out_sum = jnp.dot(shard_piece, down_local, preferred_element_type=jnp.float32)
    grad_block = lax.dot_general(
        shard_piece, grad_rows, (((0,), (0,)), ((), ())), preferred_element_type=jnp.float32
    )
    grad_sum = grad_block
    out_sum, grad_sum = (out_sum, grad_sum)
    expert_out = out_sum.astype(jnp.bfloat16).reshape(sent_rows.shape[0], capacity, slice_width)
    returned = lax.all_to_all(expert_out, "expert", split_axis=0, concat_axis=0, tiled=True)
    returned_flat = returned.reshape(experts * capacity, slice_width)
    mixed_out = (token_weight[:, None] * returned_flat[position].astype(jnp.float32)).astype(
        jnp.bfloat16
    )
    return (mixed_out, grad_sum.astype(jnp.bfloat16)[None])


def solution(mesh):
    return jax.shard_map(
        body,
        mesh=mesh,
        in_specs=(
            P("dp", None, None),
            P(None, "expert", None),
            P("expert", None),
            P("expert", None),
            P("expert", "dp"),
            P(),
            P("expert", None, "dp"),
            P("expert", None, "dp"),
            P("expert", None, "dp"),
            P("expert", "dp"),
        ),
        out_specs=(P("expert", "dp"), P("expert", None, "dp")),
        check_vma=False,
    )
```

profile of v0, /device:TPU:13, one launch (start us, length us, event | category | flops | bytes accessed | tf_op | source)
XLA Modules:
  0.0 184.4 jit_solution(7512770705820136966)
XLA Ops:
  9.9 8.8 %all_gather.12 = bf16[4,64,1152]{2,1,0:T(8,128)(2,1)S(1)} all-gather(bf16[2,64,1152]{2,1,0:T(8,128)(2,1)} %param.10), channel_id=1, replica_groups=mesh['dp'=2,'expert'=16] {'dp'}, dimensions={0}, use_global_device_ids=true | all-gather | bytes 884736 | tf_op jit(solution)/shard_map/all_gather | solution.py:36
  21.1 1.4 scatter_custom_fusion
  23.7 2.6 %gather_fusion.2 = bf16[320,1024]{1,0:T(8,128)(2,1)} fusion(bf16[256,1024]{1,0:T(8,128)(2,1)S(1)} %multiply_convert_fusion, s32[1024]{0:T(1024)S(1)} %pad_clamp_fusion.1), kind=kCustom, calls=%fused_computation.2 | custom fusion | bytes 1312000 | tf_op jit(solution)/shard_map/gather | solution.py:65
  26.4 2.0 %gather.17 = bf16[16,20,1024]{2,1,0:T(8,128)(2,1)} reshape(bf16[320,1024]{1,0:T(8,128)(2,1)} %gather_fusion.2) | data formatting | bytes 1310720 | tf_op jit(solution)/shard_map/gather | solution.py:65
  28.5 25.1 %all-gather.4.cloned.1.call-done = bf16[1152,1024]{1,0:T(8,128)(2,1)} async-done(((bf16[72,1024]{1,0:T(8,128)(2,1)}), bf16[1152,1024]{1,0:T(8,128)(2,1)}) %all-gather.4.cloned.1.call-update) | async-done | bytes 2359312 | tf_op jit(solution)/shard_map/all_gather | solution.py:44
  53.6 3.5 %fusion.19 = (f32[256]{0:T(256)S(1)}, bf16[256,1024]{1,0:T(8,128)(2,1)}) fusion(bf16[256,1152]{1,0:T(8,128)(2,1)} %bitcast.56, bf16[1152,1024]{1,0:T(8,128)(2,1)} %all-gather.4.cloned.1.call-done), kind=kOutput, calls=%fused_computation.20 | convolution fusion | flops 605028096 | bytes 3474432 | tf_op jit(solution)/shard_map/dot_general | solution.py:42
  57.1 3.8 %psum.7 = f32[256]{0:T(256)S(1)} all-reduce(f32[256]{0:T(256)S(1)} %get-tuple-element.4), channel_id=1, replica_groups=mesh['dp'=2,'expert'=16] {'dp'}, use_global_device_ids=true, to_apply=%region_5.6 | all-reduce | flops 256 | bytes 2048 | tf_op jit(solution)/shard_map/psum | solution.py:48
  62.1 2.6 %gather_fusion = bf16[320,1024]{1,0:T(8,128)(2,1)} fusion(bf16[256,1024]{1,0:T(8,128)(2,1)S(1)} %fusion.21, s32[1024]{0:T(1024)S(1)} %pad_clamp_fusion.1), kind=kCustom, calls=%fused_computation | custom fusion | bytes 1312000 | tf_op jit(solution)/shard_map/gather | solution.py:65
  64.7 2.0 %gather.14 = bf16[16,20,1024]{2,1,0:T(8,128)(2,1)} reshape(bf16[320,1024]{1,0:T(8,128)(2,1)} %gather_fusion) | data formatting | bytes 1310720 | tf_op jit(solution)/shard_map/gather | solution.py:65
  66.8 2.4 %broadcast_select_fusion = (bf16[16,20,1024]{2,1,0:T(8,128)(2,1)}, bf16[16,20,1024]{2,1,0:T(8,128)(2,1)S(1)}) fusion(bf16[16,20,1024]{2,1,0:T(8,128)(2,1)} %gather.17, pred[16,20]{1,0:T(8,128)(4,1)S(1)} %broadcast_in_dim.33, bf16[16,20,1024]{2,1,0:T(8,128)(2,1)} %gather.14), kind=kLoop, calls=%fused_computation.25 | loop fusion | flops 655360 | bytes 2621760 | tf_op jit(solution)/shard_map/jit(_where)/select_n | solution.py:65
  69.2 25.4 %all_to_all.15 = bf16[16,20,1024]{2,1,0:T(8,128)(2,1)} all-to-all(bf16[16,20,1024]{2,1,0:T(8,128)(2,1)S(1)} %get-tuple-element.3), channel_id=1, replica_groups=mesh['dp'=2,'expert'=16] {'expert'}, dimensions={0} | all-to-all | bytes 1310720 | tf_op jit(solution)/shard_map/all_to_all | solution.py:71
  94.5 2.0 %reshape.57 = bf16[320,1024]{1,0:T(8,128)(2,1)} reshape(bf16[16,20,1024]{2,1,0:T(8,128)(2,1)} %all_to_all.15) | data formatting | bytes 1310720 | tf_op jit(solution)/shard_map/reshape | solution.py:75
  96.5 4.5 %all-to-all-start.2 = ((bf16[16,20,1024]{2,1,0:T(8,128)(2,1)}), bf16[16,20,1024]{2,1,0:T(8,128)(2,1)}, u32[]{:S(2)}, u32[]{:S(2)}) async-start(bf16[16,20,1024]{2,1,0:T(8,128)(2,1)} %get-tuple-element.2), calls=%async_computation.2 | async-start | bytes 1572864 | tf_op jit(solution)/shard_map/all_to_all | solution.py:72
  101.0 17.8 %all-gather.6.cloned.1.call-done = bf16[320,2048]{1,0:T(8,128)(2,1)} async-done(((bf16[320,1024]{1,0:T(8,128)(2,1)}), bf16[320,2048]{1,0:T(8,128)(2,1)}) %all-gather.6.cloned.1.call-update) | async-done | bytes 1310736 | tf_op jit(solution)/shard_map/all_gather | solution.py:75
  118.8 3.6 %fusion.5 = f32[320,704]{1,0:T(8,128)S(1)} fusion(bf16[320,2048]{1,0:T(8,128)(2,1)} %all-gather.6.cloned.1.call-done, bf16[1,2048,704]{1,2,0:T(8,128)(2,1)} %param.16), kind=kOutput, calls=%fused_computation.10 | convolution fusion | flops 922746880 | bytes 5095424 | tf_op jit(solution)/shard_map/dot_general | solution.py:77
  123.7 12.9 %all-gather = bf16[2,704,320]{1,2,0:T(8,128)(2,1)S(1)} all-gather(bf16[1,704,320]{1,2,0:T(8,128)(2,1)S(1)} %fusion.16), channel_id=1, replica_groups=mesh['dp'=2,'expert'=16] {'dp'}, dimensions={0}, use_global_device_ids=true | all-gather | bytes 1351680 | tf_op jit(solution)/shard_map/all_gather | solution.py:81
  136.7 2.0 %copy.20 = bf16[2,704,320]{1,0,2:T(2,128)(2,1)} copy(bf16[2,704,320]{1,2,0:T(8,128)(2,1)S(1)} %all-gather) | data formatting | bytes 1802240 | tf_op jit(solution)/shard_map/all_gather | solution.py:81
  138.6 3.4 %reshape.96 = bf16[1408,320]{0,1:T(8,128)(2,1)} reshape(bf16[2,704,320]{1,0,2:T(2,128)(2,1)} %copy.20) | data formatting | bytes 1802240
  142.1 2.4 %fusion.10 = bf16[320,1024]{1,0:T(8,128)(2,1)S(1)} fusion(bf16[1408,320]{0,1:T(8,128)(2,1)} %reshape.96, bf16[1,1408,1024]{2,1,0:T(8,128)(2,1)S(1)} %copy-done), kind=kOutput, calls=%fused_computation.14 | convolution fusion | flops 923074560 | bytes 4440064 | tf_op jit(solution)/shard_map/dot_general | solution.py:82
  145.4 7.3 %all-to-all-start.1 = ((bf16[16,20,1024]{2,1,0:T(8,128)(2,1)}), bf16[16,20,1024]{2,1,0:T(8,128)(2,1)}, u32[]{:S(2)}, u32[]{:S(2)}) async-start(bf16[16,20,1024]{2,1,0:T(8,128)(2,1)} %reshape.58), calls=%async_computation.1 | async-start | bytes 1572864 | tf_op jit(solution)/shard_map/all_to_all | solution.py:89
  154.0 4.4 %fusion = bf16[1,1408,1024]{2,1,0:T(8,128)(2,1)} fusion(bf16[1408,320]{0,1:T(8,128)(2,1)} %reshape.96, bf16[320,1024]{1,0:T(8,128)(2,1)S(1)} %reshape.60), kind=kOutput, calls=%fused_computation.5 | convolution fusion | flops 924188672 | bytes 4440064 | tf_op jit(solution)/shard_map/dot_general | solution.py:83
  158.4 13.9 %all-to-all-done.1 = bf16[16,20,1024]{2,1,0:T(8,128)(2,1)} async-done(((bf16[16,20,1024]{2,1,0:T(8,128)(2,1)}), bf16[16,20,1024]{2,1,0:T(8,128)(2,1)}, u32[]{:S(2)}, u32[]{:S(2)}) %all-to-all-start.1) | async-done | bytes 655392 | tf_op jit(solution)/shard_map/all_to_all | solution.py:89
  173.6 2.0 %gather_fusion.1 = bf16[256,1024]{1,0:T(8,128)(2,1)} fusion(bf16[320,1024]{1,0:T(8,128)(2,1)S(1)} %reshape.59, s32[1024]{0:T(1024)S(1)} %pad_clamp_fusion), kind=kCustom, calls=%fused_computation.1 | custom fusion | bytes 1049600 | tf_op jit(solution)/shard_map/gather | solution.py:91
  175.6 2.0 %multiply_convert_fusion.1 = bf16[256,1024]{1,0:T(8,128)(2,1)} fusion(bf16[256,1024]{1,0:T(8,128)(2,1)} %gather_fusion.1, f32[256]{0:T(256)S(1)} %bitcast.60), kind=kLoop, calls=%fused_computation.24 | loop fusion | flops 786432 | bytes 1049600 | tf_op jit(solution)/shard_map/convert_element_type | solution.py:91
  (42 shorter events, 12.5 us)
Async XLA Ops:
  7.2 134.9 %copy-start = (bf16[1,1408,1024]{2,1,0:T(8,128)(2,1)S(1)}, bf16[1,1408,1024]{2,1,0:T(8,128)(2,1)}, u32[]{:S(2)}) copy-start(bf16[1,1408,1024]{2,1,0:T(8,128)(2,1)} %param.18) | copy-start | bytes 8650756
  7.2 13.0 %copy-start.1 = (s32[256,1]{0,1:T(1,128)S(1)}, s32[256,1]{0,1:T(1,128)}, u32[]{:S(2)}) copy-start(s32[256,1]{0,1:T(1,128)} %param.12) | copy-start | bytes 3076
  7.2 15.3 %copy-start.2 = (f32[256,1]{0,1:T(1,128)S(1)}, f32[256,1]{0,1:T(1,128)}, u32[]{:S(2)}) copy-start(f32[256,1]{0,1:T(1,128)} %param.13) | copy-start | bytes 3076
  7.2 46.4 %all-gather.4.cloned.1.call-start = ((), (), s32[]{:S(2)}) async-start(), calls=%async_computation.3 | async-start | bytes 2506752 | tf_op jit(solution)/shard_map/all_gather | solution.py:44
  7.9 110.9 %all-gather.6.cloned.1.call-start = ((), (), s32[]{:S(2)}) async-start(), calls=%async_computation.4 | async-start | bytes 1966080 | tf_op jit(solution)/shard_map/all_gather | solution.py:75
  28.5 32.4 %dynamic-slice-start = ((f32[2048]{0:T(1024)}, s32[]{:T(128)}), f32[1024]{0:T(1024)S(1)}, s32[]{:S(2)}) async-start(f32[2048]{0:T(1024)} %param.15, s32[]{:T(128)} %select_n.20), calls=%async_computation.5 | async-start | bytes 8704 | tf_op jit(solution)/shard_map/dynamic_slice | solution.py:47
  96.5 48.9 %all-to-all-start.2 = ((bf16[16,20,1024]{2,1,0:T(8,128)(2,1)}), bf16[16,20,1024]{2,1,0:T(8,128)(2,1)}, u32[]{:S(2)}, u32[]{:S(2)}) async-start(bf16[16,20,1024]{2,1,0:T(8,128)(2,1)} %get-tuple-element.2), calls=%async_computation.2 | async-start | bytes 1572864 | tf_op jit(solution)/shard_map/all_to_all | solution.py:72
  118.8 3.6 %copy-start.3 = (bf16[1,2048,704]{1,2,0:T(8,128)(2,1)S(1)}, bf16[1,2048,704]{1,2,0:T(8,128)(2,1)}, u32[]{:S(2)}) copy-start(bf16[1,2048,704]{1,2,0:T(8,128)(2,1)} %param.17) | copy-start | bytes 8650756
  118.8 3.6 %copy-start.4 = (bf16[320,2048]{1,0:T(8,128)(2,1)S(1)}, bf16[320,2048]{1,0:T(8,128)(2,1)}, u32[]{:S(2)}) copy-start(bf16[320,2048]{1,0:T(8,128)(2,1)} %all-gather.6.cloned.1.call-done) | copy-start | bytes 3932164
  145.4 26.9 %all-to-all-start.1 = ((bf16[16,20,1024]{2,1,0:T(8,128)(2,1)}), bf16[16,20,1024]{2,1,0:T(8,128)(2,1)}, u32[]{:S(2)}, u32[]{:S(2)}) async-start(bf16[16,20,1024]{2,1,0:T(8,128)(2,1)} %reshape.58), calls=%async_computation.1 | async-start | bytes 1572864 | tf_op jit(solution)/shard_map/all_to_all | solution.py:89
Sparse Core Ops, SparseCore 0:
  10.3 43.2 all-gather.3
  96.7 22.1 all-gather.5
where the time goes:
time: 186 us; the launch traced here: 184 us
  waiting for transfers between devices  57.5 us (31%)
  blocking collectives  50.8 us (27%)
  local copies, waits for them, and re-layouts  25.4 us (14%)
  matrix products  15.8 us (8%)
  between operations  14.2 us (8%)
  starting transfers between devices  11.8 us (6%)
  other arithmetic  8.93 us (5%)
    all_to_all x1, blocking collectives, body(): lax.all_to_all(arrange(source_rows), 'expert', split_axis=0, concat_axis=...  25.4 us
    all_gather x1, waiting for transfers between devices, body(): lax.all_gather(proj_weight, 'expert', axis=0, tiled=True)  25.1 us
    all_gather x1, waiting for transfers between devices, body(): lax.all_gather(sent_rows.reshape(slot_count, slice_width), 'dp', axis=1,...  17.8 us
    all_to_all x1, waiting for transfers between devices, body(): lax.all_to_all(expert_out, 'expert', split_axis=0, concat_axis=0, tiled=T...  13.9 us
    all_gather x1, blocking collectives, body(): shard_piece = lax.all_gather(hidden, 'dp', axis=1, tiled=True)  12.9 us
    gather x4, local copies, waits for them, and re-layouts, arrange(): row_block[source_row]  9.29 us
    all_gather x1, blocking collectives, body(): shard_piece = lax.all_gather(cache, 'dp', axis=0, tiled=True)  8.75 us
    all_to_all x1, starting transfers between devices, body(): lax.all_to_all(expert_out, 'expert', split_axis=0, concat_axis=0, tiled=T...  7.28 us
  transfers between devices with their start and end apart: 4, of which 3 were waited for; matrix products, arithmetic and copies ran while one was open for 17% of the time, Pallas kernels for 0%

commit v1 on v0

v1 whole, which is shorter than its diff:
```python
import jax
import jax.numpy as jnp
from jax import lax
from jax.sharding import PartitionSpec as P

BF = jnp.bfloat16
F32 = jnp.float32


def dot(a, b, dims=((1,), (0,))):
    return lax.dot_general(a, b, (dims, ((), ())), preferred_element_type=F32)


def body(
    cache,
    requests,
    routes,
    combine_weight,
    proj_weight,
    norm_gain,
    gate_weight,
    up_weight,
    down_weight,
    cotangent,
):
    width = cotangent.shape[1]
    n_expert = lax.axis_size("expert")
    experts = n_expert * gate_weight.shape[0]
    block, feat = cache.shape[1:]

    feats = lax.all_gather(cache, "dp", axis=0, tiled=True).reshape(-1, feat)
    lanes = width // n_expert
    piece = lax.all_to_all(
        proj_weight.reshape(-1, n_expert, lanes), "expert", split_axis=1, concat_axis=0, tiled=True
    ).reshape(feat, lanes)
    part = dot(feats, piece).astype(BF)
    projected = lax.all_gather(part, ("dp", "expert"), axis=1, tiled=True)
    values = projected.astype(F32)
    mean_square = jnp.mean(values * values, axis=1)
    table = (values * lax.rsqrt(mean_square + 1e-06)[:, None] * norm_gain[None, :]).astype(BF)
    table_rows = table.shape[0]

    token_row = (
        requests.reshape(-1)[:, None] * block + jnp.arange(block, dtype=jnp.int32)[None, :]
    ).reshape(-1)
    tokens = token_row.shape[0]
    capacity = max(2, 5 * tokens // (4 * experts))
    expert_id = routes[:, 0]
    order = jnp.arange(tokens, dtype=jnp.int32)
    earlier = (expert_id[:, None] == expert_id[None, :]) & (order[None, :] < order[:, None])
    slot_rank = jnp.sum(earlier.astype(jnp.int32), axis=1)
    position = expert_id * capacity + slot_rank
    hit = jnp.arange(experts * capacity, dtype=jnp.int32)[:, None] == position[None, :]
    pick = hit.astype(BF)
    slot_row = jnp.sum(jnp.where(hit, token_row[None, :] + 1, 0), axis=1) - 1

    token_weight = combine_weight[:, 0]
    scaled_grad = (token_weight[:, None] * cotangent.astype(F32)).astype(BF)
    sent = dot(pick, scaled_grad).astype(BF).reshape(experts, capacity, width)
    grad_rows = lax.all_to_all(sent, "expert", split_axis=0, concat_axis=0, tiled=True)
    grad_rows = grad_rows.reshape(-1, width)
    rows = lax.all_to_all(
        slot_row.reshape(experts, capacity), "expert", split_axis=0, concat_axis=0, tiled=True
    ).reshape(-1)
    select = (rows[:, None] == jnp.arange(table_rows, dtype=jnp.int32)[None, :]).astype(BF)

    gate_act = dot(table, gate_weight[0])
    up_act = dot(table, up_weight[0])
    half = (jax.nn.silu(gate_act) * up_act).astype(BF)
    hidden = lax.all_gather(half, "dp", axis=1, tiled=True)
    out_rows = dot(hidden, down_weight[0]).astype(BF)
    sent_out = dot(select, out_rows).astype(BF).reshape(-1, capacity, width)
    hidden_rows = dot(select, hidden).astype(BF)
    down_grad = dot(hidden_rows, grad_rows, ((0,), (0,))).astype(BF)
    returned = lax.all_to_all(sent_out, "expert", split_axis=0, concat_axis=0, tiled=True)
    token_out = dot(pick, returned.reshape(experts * capacity, width), ((0,), (0,)))
    mixed = (token_weight[:, None] * token_out).astype(BF)
    return mixed, down_grad[None]


def solution(mesh):
    return jax.shard_map(
        body,
        mesh=mesh,
        in_specs=(
            P("dp", None, None),
            P(None, "expert", None),
            P("expert", None),
            P("expert", None),
            P("expert", "dp"),
            P(),
            P("expert", None, "dp"),
            P("expert", None, "dp"),
            P("expert", None, "dp"),
            P("expert", "dp"),
        ),
        out_specs=(P("expert", "dp"), P("expert", None, "dp")),
        check_vma=False,
    )
```

time: 186 us -> 145 us (0.78)
  blocking collectives: 50.8 us -> 19.7 us
  local copies, waits for them, and re-layouts: 25.4 us -> 11.7 us
  starting transfers between devices: 11.8 us -> 25.3 us
  other arithmetic: 8.93 us -> 2.68 us
  waiting for transfers between devices: 57.5 us -> 54.1 us
    all_to_all x1 -> x0, blocking collectives: 25.4 us -> none  [body(): lax.all_to_all(arrange(source_rows), 'expert', split_axis=0, concat_axis=...]
    all_to_all x2 -> x4, starting transfers between devices: 11.8 us -> 25.3 us  [the longest x1 6.85 us: body(): lax.all_to_all(slot_row.reshape(experts, capacity), 'expert', split_axis=...]
    gather x5 -> x0, local copies, waits for them, and re-layouts: 11.3 us -> none  [the longest x4 9.29 us: arrange(): row_block[source_row]]
    all_gather x2 -> x1, waiting for transfers between devices: 42.9 us -> 38.1 us  [body(): projected = lax.all_gather(part, ('dp', 'expert'), axis=1, tiled=True)]
    convert_element_type x4 -> x0, other arithmetic: 4.42 us -> none  [the longest x1 1.99 us: body(): (token_weight[:, None] * returned_flat[position].astype(jnp.float32)).ast...]
    unnamed x12 -> x14, local copies, waits for them, and re-layouts: 3.98 us -> 0.04 us
    psum x1 -> x0, blocking collectives: 3.77 us -> none  [body(): sum_squares = lax.psum(local_squares(projected), 'dp')]
    reshape x4 -> x6, local copies, waits for them, and re-layouts: 5.52 us -> 8.33 us  [the longest x1 1.9 us: body(): proj_weight.reshape(-1, n_expert, lanes)]
  transfers between devices with their start and end apart: 4 -> 5, of which waited for: 3 -> 3; matrix products, arithmetic and copies ran while one was open for 17% -> 14% of each run, Pallas kernels for 0% -> 0%
where the time goes in v1:
time: 145 us; the launch traced here: 144 us
  waiting for transfers between devices  54.1 us (37%)
  starting transfers between devices  25.3 us (17%)
  blocking collectives  19.7 us (14%)
  matrix products  16 us (11%)
  between operations  14.2 us (10%)
  local copies, waits for them, and re-layouts  11.7 us (8%)
  other arithmetic  2.68 us (2%)
    all_gather x1, waiting for transfers between devices, body(): projected = lax.all_gather(part, ('dp', 'expert'), axis=1, tiled=True)  38.1 us
    dot_general x7, matrix products, dot(): return lax.dot_general(a, b, (dims, ((), ())), preferred_element_type=F32)  16 us
    all_to_all x1, waiting for transfers between devices, body(): lax.all_to_all(sent_out, 'expert', split_axis=0, concat_axis=0, tiled=True)  13.8 us
    all_gather x1, blocking collectives, body(): hidden = lax.all_gather(half, 'dp', axis=1, tiled=True)  10.6 us
    all_gather x1, blocking collectives, body(): feats = lax.all_gather(cache, 'dp', axis=0, tiled=True).reshape(-1, feat)  9.12 us
    all_to_all x1, starting transfers between devices, body(): lax.all_to_all(slot_row.reshape(experts, capacity), 'expert', split_axis=...  6.85 us
    all_to_all x1, starting transfers between devices, body(): lax.all_to_all(proj_weight.reshape(-1, n_expert, lanes), 'expert', split_...  6.58 us
    all_to_all x1, starting transfers between devices, body(): lax.all_to_all(sent_out, 'expert', split_axis=0, concat_axis=0, tiled=True)  6.02 us
  transfers between devices with their start and end apart: 5, of which 3 were waited for; matrix products, arithmetic and copies ran while one was open for 14% of the time, Pallas kernels for 0%

profile of v1, /device:TPU:13, one launch (start us, length us, event | category | flops | bytes accessed | tf_op | source)
XLA Modules:
  0.0 143.7 jit_solution(15097482984221297119)
XLA Ops:
  7.2 1.9 %copy.17 = bf16[72,1024]{0,1:T(8,128)(2,1)} copy(bf16[72,1024]{1,0:T(8,128)(2,1)} %param.14) | data formatting | bytes 294912 | tf_op jit(solution)/shard_map/reshape | solution.py:34
  9.1 6.6 %all-to-all-start.1 = ((bf16[72,16,64]{0,2,1:T(8,128)(2,1)}), bf16[72,16,64]{0,2,1:T(8,128)(2,1)}, u32[]{:S(2)}, u32[]{:S(2)}) async-start(bf16[72,16,64]{0,2,1:T(8,128)(2,1)} %bitcast.3), calls=%async_computation.1 | async-start | bytes 524288 | tf_op jit(solution)/shard_map/all_to_all | solution.py:33
  15.7 9.1 %all_gather.9 = bf16[4,64,1152]{2,1,0:T(8,128)(2,1)S(1)} all-gather(bf16[2,64,1152]{2,1,0:T(8,128)(2,1)} %param.10), channel_id=1, replica_groups=mesh['dp'=2,'expert'=16] {'dp'}, dimensions={0}, use_global_device_ids=true | all-gather | bytes 884736 | tf_op jit(solution)/shard_map/all_gather | solution.py:31
  24.9 1.8 %copy.16 = bf16[16,72,1,64]{1,0,3,2:T(8,128)(2,1)} copy(bf16[16,72,1,64]{1,3,0,2:T(8,128)(2,1)} %bitcast.5) | data formatting | bytes 294912 | tf_op jit(solution)/shard_map/all_to_all | solution.py:33
  26.7 1.9 %reshape.87 = bf16[1152,64]{0,1:T(8,128)(2,1)} reshape(bf16[16,72,1,64]{1,0,3,2:T(8,128)(2,1)} %copy.16) | data formatting | bytes 294912 | tf_op jit(solution)/shard_map/reshape | solution.py:35
  28.6 1.8 %convolution_convert_fusion.4 = bf16[256,64]{0,1:T(8,128)(2,1)} fusion(bf16[256,1152]{1,0:T(8,128)(2,1)S(1)} %bitcast.36, bf16[1152,64]{0,1:T(8,128)(2,1)} %reshape.87), kind=kOutput, calls=%fused_computation.21 | convolution fusion | flops 37765120 | bytes 770048 | tf_op jit(solution)/shard_map/dot_general | solution.py:11
  31.8 6.8 %all-to-all-start = ((s32[16,1,20]{2,1,0:T(1,128)}), s32[16,1,20]{2,1,0:T(1,128)S(1)}, u32[]{:S(2)}, u32[]{:S(2)}) async-start(s32[16,1,20]{2,1,0:T(1,128)} %sub.7), calls=%async_computation | async-start | bytes 16384 | tf_op jit(solution)/shard_map/all_to_all | solution.py:62
  38.6 1.5 %convolution_convert_fusion.2 = bf16[320,1024]{1,0:T(8,128)(2,1)S(1)} fusion(bf16[256,1024]{1,0:T(8,128)(2,1)} %param.19, f32[256]{0:T(256)S(1)} %bitcast.39, s32[256]{0:T(256)S(1)} %multiply_add_fusion), kind=kOutput, calls=%fused_computation.15 | convolution fusion | flops 168968192 | bytes 1181696 | tf_op jit(solution)/shard_map/dot_general | solution.py:11
  40.1 1.0 reshape.90
  41.1 2.2 %all-to-all-done = s32[16,1,20]{2,1,0:T(1,128)S(1)} async-done(((s32[16,1,20]{2,1,0:T(1,128)}), s32[16,1,20]{2,1,0:T(1,128)S(1)}, u32[]{:S(2)}, u32[]{:S(2)}) %all-to-all-start) | async-done | bytes 1312 | tf_op jit(solution)/shard_map/all_to_all | solution.py:62
  43.3 5.9 %all-to-all-start.3 = ((bf16[16,20,1024]{2,1,0:T(8,128)(2,1)}), bf16[16,20,1024]{2,1,0:T(8,128)(2,1)}, u32[]{:S(2)}, u32[]{:S(2)}) async-start(bf16[16,20,1024]{2,1,0:T(8,128)(2,1)} %reshape.90), calls=%async_computation.3 | async-start | bytes 1572864 | tf_op jit(solution)/shard_map/all_to_all | solution.py:60
  50.5 38.1 %all-gather.2.cloned.1.call-done = bf16[256,2048]{0,1:T(8,128)(2,1)} async-done(((bf16[256,64]{0,1:T(8,128)(2,1)}), bf16[256,2048]{0,1:T(8,128)(2,1)}) %all-gather.2.cloned.1.call-update) | async-done | bytes 1048592 | tf_op jit(solution)/shard_map/all_gather | solution.py:37
  88.7 1.5 %fusion.7 = f32[256]{0:T(256)S(1)} fusion(bf16[256,2048]{0,1:T(8,128)(2,1)} %all-gather.2.cloned.1.call-done), kind=kLoop, calls=%fused_computation.11 | loop fusion | flops 1572608 | bytes 1049600 | tf_op jit(solution)/shard_map/reduce_sum | solution.py:39
  90.3 3.3 %fusion.5 = f32[256,704]{0,1:T(8,128)S(1)} fusion(bf16[1,2048,704]{1,2,0:T(8,128)(2,1)} %param.16, bf16[256,2048]{0,1:T(8,128)(2,1)} %all-gather.2.cloned.1.call-done, f32[2048]{0:T(1024)} %param.15, f32[256]{0:T(256)S(1)} %add_rsqrt_fusion), kind=kOutput, calls=%fused_computation.6 | convolution fusion | flops 740294656 | bytes 4662272 | tf_op jit(solution)/shard_map/dot_general | solution.py:11
  93.6 1.0 fusion.17
  94.6 10.6 %all_gather.11 = bf16[256,1408]{0,1:T(8,128)(2,1)} all-gather(bf16[256,704]{0,1:T(8,128)(2,1)S(1)} %fusion.17), channel_id=1, replica_groups=mesh['dp'=2,'expert'=16] {'dp'}, dimensions={1}, use_global_device_ids=true | all-gather | bytes 1081344 | tf_op jit(solution)/shard_map/all_gather | solution.py:70
  105.2 2.3 %convolution_convert_fusion.3 = bf16[320,1024]{1,0:T(8,128)(2,1)S(1)} fusion(bf16[256,1408]{0,1:T(8,128)(2,1)} %all_gather.11, bf16[1,1408,1024]{2,1,0:T(8,128)(2,1)S(1)} %copy-done, s32[320]{0:T(512)S(1)} %eq.47), kind=kOutput, calls=%fused_computation.16 | convolution fusion | flops 906641408 | bytes 4261120 | tf_op jit(solution)/shard_map/dot_general | solution.py:11
  107.6 1.0 reshape.88
  108.6 6.0 %all-to-all-start.2 = ((bf16[16,20,1024]{2,1,0:T(8,128)(2,1)}), bf16[16,20,1024]{2,1,0:T(8,128)(2,1)}, u32[]{:S(2)}, u32[]{:S(2)}) async-start(bf16[16,20,1024]{2,1,0:T(8,128)(2,1)} %reshape.88), calls=%async_computation.2 | async-start | bytes 1572864 | tf_op jit(solution)/shard_map/all_to_all | solution.py:75
  114.6 1.2 reshape.91
  115.9 4.7 %fusion = bf16[1,1408,1024]{2,1,0:T(8,128)(2,1)} fusion(bf16[320,1024]{1,0:T(8,128)(2,1)S(1)} %reshape.91, bf16[256,1408]{0,1:T(8,128)(2,1)} %all_gather.11, s32[320]{0:T(512)S(1)} %eq.47), kind=kOutput, calls=%fused_computation.1 | convolution fusion | flops 1155407872 | bytes 4261120 | tf_op jit(solution)/shard_map/dot_general | solution.py:11
  120.5 13.8 %all-to-all-done.2 = bf16[16,20,1024]{2,1,0:T(8,128)(2,1)} async-done(((bf16[16,20,1024]{2,1,0:T(8,128)(2,1)}), bf16[16,20,1024]{2,1,0:T(8,128)(2,1)}, u32[]{:S(2)}, u32[]{:S(2)}) %all-to-all-start.2) | async-done | bytes 655392 | tf_op jit(solution)/shard_map/all_to_all | solution.py:75
  134.3 1.2 reshape.89
  135.6 1.3 fusion.13
  (31 shorter events, 2.8 us)
Async XLA Ops:
  7.2 98.0 %copy-start = (bf16[1,1408,1024]{2,1,0:T(8,128)(2,1)S(1)}, bf16[1,1408,1024]{2,1,0:T(8,128)(2,1)}, u32[]{:S(2)}) copy-start(bf16[1,1408,1024]{2,1,0:T(8,128)(2,1)} %param.18) | copy-start | bytes 8650756
  7.2 23.3 %copy-start.4 = (s32[2,1,2]{2,1,0:T(1,128)S(1)}, s32[2,1,2]{2,1,0:T(1,128)}, u32[]{:S(2)}) copy-start(s32[2,1,2]{2,1,0:T(1,128)} %param.11) | copy-start | bytes 52
  7.2 23.5 %copy-start.2 = (s32[256,1]{0,1:T(1,128)S(1)}, s32[256,1]{0,1:T(1,128)}, u32[]{:S(2)}) copy-start(s32[256,1]{0,1:T(1,128)} %param.12) | copy-start | bytes 3076
  7.2 31.4 %copy-start.3 = (f32[256,1]{0,1:T(1,128)S(1)}, f32[256,1]{0,1:T(1,128)}, u32[]{:S(2)}) copy-start(f32[256,1]{0,1:T(1,128)} %param.13) | copy-start | bytes 3076
  9.1 15.8 %all-to-all-start.1 = ((bf16[72,16,64]{0,2,1:T(8,128)(2,1)}), bf16[72,16,64]{0,2,1:T(8,128)(2,1)}, u32[]{:S(2)}, u32[]{:S(2)}) async-start(bf16[72,16,64]{0,2,1:T(8,128)(2,1)} %bitcast.3), calls=%async_computation.1 | async-start | bytes 524288 | tf_op jit(solution)/shard_map/all_to_all | solution.py:33
  15.7 73.0 %all-gather.2.cloned.1.call-start = ((), (), s32[]{:S(2)}) async-start(), calls=%async_computation.4 | async-start | bytes 1081344 | tf_op jit(solution)/shard_map/all_gather | solution.py:37
  31.8 11.5 %all-to-all-start = ((s32[16,1,20]{2,1,0:T(1,128)}), s32[16,1,20]{2,1,0:T(1,128)S(1)}, u32[]{:S(2)}, u32[]{:S(2)}) async-start(s32[16,1,20]{2,1,0:T(1,128)} %sub.7), calls=%async_computation | async-start | bytes 16384 | tf_op jit(solution)/shard_map/all_to_all | solution.py:62
  43.3 65.3 %all-to-all-start.3 = ((bf16[16,20,1024]{2,1,0:T(8,128)(2,1)}), bf16[16,20,1024]{2,1,0:T(8,128)(2,1)}, u32[]{:S(2)}, u32[]{:S(2)}) async-start(bf16[16,20,1024]{2,1,0:T(8,128)(2,1)} %reshape.90), calls=%async_computation.3 | async-start | bytes 1572864 | tf_op jit(solution)/shard_map/all_to_all | solution.py:60
  90.2 3.3 %copy-start.1 = (bf16[256,2048]{0,1:T(8,128)(2,1)S(1)}, bf16[256,2048]{0,1:T(8,128)(2,1)}, u32[]{:S(2)}) copy-start(bf16[256,2048]{0,1:T(8,128)(2,1)} %all-gather.2.cloned.1.call-done) | copy-start | bytes 3145732
  90.2 3.3 %copy-start.5 = (bf16[1,2048,704]{1,2,0:T(8,128)(2,1)S(1)}, bf16[1,2048,704]{1,2,0:T(8,128)(2,1)}, u32[]{:S(2)}) copy-start(bf16[1,2048,704]{1,2,0:T(8,128)(2,1)} %param.17) | copy-start | bytes 8650756
  90.2 3.3 %copy-start.6 = (f32[2048]{0:T(1024)S(1)}, f32[2048]{0:T(1024)}, u32[]{:S(2)}) copy-start(f32[2048]{0:T(1024)} %param.15) | copy-start | bytes 24580
  108.6 25.7 %all-to-all-start.2 = ((bf16[16,20,1024]{2,1,0:T(8,128)(2,1)}), bf16[16,20,1024]{2,1,0:T(8,128)(2,1)}, u32[]{:S(2)}, u32[]{:S(2)}) async-start(bf16[16,20,1024]{2,1,0:T(8,128)(2,1)} %reshape.88), calls=%async_computation.2 | async-start | bytes 1572864 | tf_op jit(solution)/shard_map/all_to_all | solution.py:75
Sparse Core Ops, SparseCore 0:
  30.6 58.0 all-gather.1

commit v2 on v1

--- a/solution.py
+++ b/solution.py
@@ -1,7 +1,13 @@
+import functools
+
 import jax
 import jax.numpy as jnp
 from jax import lax
+from jax.experimental import pallas as pl
+from jax.experimental.pallas import tpu as pltpu
 from jax.sharding import PartitionSpec as P
+
+MESH = pl.DeviceIdType.MESH
 
 BF = jnp.bfloat16
 F32 = jnp.float32
@@ -9,6 +15,246 @@
 
 def dot(a, b, dims=((1,), (0,))):
     return lax.dot_general(a, b, (dims, ((), ())), preferred_element_type=F32)
+
+
+def loop(start, stop, step):
+    def run(i, carry):
+        step(i)
+        return carry
+
+    lax.fori_loop(start, stop, run, 0)
+
+
+def remote(src, dst, send_sem, recv_sem, device):
+    return pltpu.make_async_remote_copy(
+        src_ref=src,
+        dst_ref=dst,
+        send_sem=send_sem,
+        recv_sem=recv_sem,
+        device_id=device,
+        device_id_type=MESH,
+    )
+
+
+def table_kernel(
+    n_dp,
+    n_expert,
+    feat_ref,
+    proj_ref,
+    rows_ref,
+    tab_ref,
+    got_ref,
+    held,
+    proj_send,
+    proj_recv,
+    row_send,
+    row_recv,
+    dp_send,
+    dp_recv,
+    far_send,
+    far_recv,
+    near_send,
+    near_recv,
+):
+    y = lax.axis_index("dp")
+    e = lax.axis_index("expert")
+    groups = n_expert // n_dp
+    near = 4 if n_expert % 4 == 0 else 1
+    far = n_expert // near
+    a, b = e // near, e % near
+    n = n_dp * n_expert
+    me = y * n_expert + e
+    other = ((y + 1) % n_dp, e)
+
+    barrier = pltpu.get_barrier_semaphore()
+
+    def greet(i):
+        t = (me + i) % n
+        pl.semaphore_signal(
+            barrier, inc=1, device_id=(t // n_expert, t % n_expert), device_id_type=MESH
+        )
+
+    loop(1, n, greet)
+    pl.semaphore_wait(barrier, n - 1)
+
+    mine = e // groups == y
+
+    def send_proj(dy, dj):
+        j = (e + dj) % groups
+        return remote(
+            proj_ref.at[j],
+            held.at[e],
+            proj_send.at[dy * groups + dj],
+            proj_recv.at[e],
+            ((y + dy) % n_dp, y * groups + j),
+        )
+
+    for dj in range(groups):
+        for dy in range(n_dp):
+            if dy == 0 and dj == 0:
+                pl.when(jnp.logical_not(mine))(lambda: send_proj(0, 0).start())
+            else:
+                send_proj(dy, dj).start()
+
+    @pl.when(mine)
+    def _():
+        held[e] = proj_ref[e % groups]
+
+    got_ref[e] = rows_ref[e]
+
+    def send_row(i):
+        t = (e + i) % n_expert
+        return remote(rows_ref.at[t], got_ref.at[e], row_send.at[i], row_recv.at[i], (y, t))
+
+    loop(1, n_expert, lambda i: send_row(i).start())
+
+    def await_proj(i):
+        s = (e + i) % n_expert
+        remote(proj_ref.at[0], held.at[s], proj_send.at[0], proj_recv.at[s], other).wait_recv()
+
+    pl.when(jnp.logical_not(mine))(lambda: await_proj(0))
+    loop(1, n_expert, await_proj)
+
+    weight = held[...].reshape(-1, held.shape[2])
+    part = jnp.dot(feat_ref[...], weight, preferred_element_type=jnp.float32)
+    tab_ref[e, y] = part.astype(jnp.bfloat16)
+
+    def over_dp(d, src):
+        return remote(
+            tab_ref.at[e, src],
+            tab_ref.at[e, src],
+            dp_send.at[d],
+            dp_recv.at[d],
+            ((y + d) % n_dp, e),
+        )
+
+    for d in range(1, n_dp):
+        over_dp(d, y).start()
+    for d in range(1, n_dp):
+        over_dp(d, (y + n_dp - d) % n_dp).wait_recv()
+
+    def to_far(d, block):
+        return remote(
+            tab_ref.at[block],
+            tab_ref.at[block],
+            far_send.at[d],
+            far_recv.at[d],
+            (y, (a + d) % far * near + b),
+        )
+
+    def to_near(d, c, block):
+        return remote(
+            tab_ref.at[block],
+            tab_ref.at[block],
+            near_send.at[d, c],
+            near_recv.at[d, c],
+            (y, a * near + (b + c) % near),
+        )
+
+    for d in range(1, far):
+        to_far(d, e).start()
+    for d in range(far):
+        block = (a + far - d) % far * near + b
+        if d:
+            to_far(d, block).wait_recv()
+        for c in range(1, near):
+            to_near(d, c, block).start()
+    for d in range(far):
+        for c in range(1, near):
+            to_near(d, c, (a + far - d) % far * near + (b + near - c) % near).wait_recv()
+
+    def await_row(i):
+        s = (e + n_expert - i) % n_expert
+        remote(
+            rows_ref.at[0], got_ref.at[s], row_send.at[i], row_recv.at[i], other
+        ).wait_recv()
+
+    loop(1, n_expert, await_row)
+    pl.when(jnp.logical_not(mine))(lambda: send_proj(0, 0).wait_send())
+    for dj in range(groups):
+        for dy in range(n_dp):
+            if dy or dj:
+                send_proj(dy, dj).wait_send()
+    loop(1, n_expert, lambda i: send_row(i).wait_send())
+    for d in range(1, n_dp):
+        over_dp(d, y).wait_send()
+    for d in range(1, far):
+        to_far(d, e).wait_send()
+    for d in range(far):
+        for c in range(1, near):
+            to_near(d, c, (a + far - d) % far * near + b).wait_send()
+
+
+def share_kernel(n_dp, half_ref, out_ref, send_sem, recv_sem):
+    y = lax.axis_index("dp")
+    e = lax.axis_index("expert")
+    barrier = pltpu.get_barrier_semaphore()
+    for d in range(1, n_dp):
+        pl.semaphore_signal(
+            barrier, inc=1, device_id=((y + d) % n_dp, e), device_id_type=MESH
+        )
+    pl.semaphore_wait(barrier, n_dp - 1)
+
+    def send(d, src):
+        return remote(
+            half_ref, out_ref.at[src], send_sem.at[d], recv_sem.at[d], ((y + d) % n_dp, e)
+        )
+
+    for d in range(1, n_dp):
+        send(d, y).start()
+    out_ref[y] = half_ref[...]
+    for d in range(1, n_dp):
+        send(d, (y + n_dp - d) % n_dp).wait_recv()
+    for d in range(1, n_dp):
+        send(d, y).wait_send()
+
+
+def in_vmem(count):
+    return [pl.BlockSpec(memory_space=pltpu.VMEM)] * count
+
+
+def make_table(n_dp, n_expert, feats, proj, rows):
+    dma = pltpu.SemaphoreType.DMA
+    near = 4 if n_expert % 4 == 0 else 1
+    far = n_expert // near
+    return pl.pallas_call(
+        functools.partial(table_kernel, n_dp, n_expert),
+        out_shape=(
+            jax.ShapeDtypeStruct((n_expert, n_dp, feats.shape[0], proj.shape[2]), BF),
+            jax.ShapeDtypeStruct(rows.shape, rows.dtype),
+        ),
+        in_specs=in_vmem(3),
+        out_specs=tuple(in_vmem(2)),
+        scratch_shapes=[
+            pltpu.VMEM((n_expert,) + proj.shape[1:], BF),
+            dma((n_expert,)),
+            dma((n_expert,)),
+            dma((n_expert,)),
+            dma((n_expert,)),
+            dma((n_dp,)),
+            dma((n_dp,)),
+            dma((far,)),
+            dma((far,)),
+            dma((far, near)),
+            dma((far, near)),
+        ],
+        compiler_params=pltpu.CompilerParams(
+            collective_id=0, has_side_effects=True, vmem_limit_bytes=48 * 2**20
+        ),
+    )(feats, proj, rows)
+
+
+def share(n_dp, half):
+    return pl.pallas_call(
+        functools.partial(share_kernel, n_dp),
+        out_shape=jax.ShapeDtypeStruct((n_dp,) + half.shape, half.dtype),
+        in_specs=in_vmem(1),
+        out_specs=in_vmem(1)[0],
+        scratch_shapes=[pltpu.SemaphoreType.DMA((n_dp,)), pltpu.SemaphoreType.DMA((n_dp,))],
+        compiler_params=pltpu.CompilerParams(
+            collective_id=1, has_side_effects=True, vmem_limit_bytes=32 * 2**20
+        ),
+    )(half)
 
 
 def body(
@@ -26,19 +272,10 @@
     width = cotangent.shape[1]
     n_expert = lax.axis_size("expert")
     experts = n_expert * gate_weight.shape[0]
-    block, feat = cache.shape[1:]
-
-    feats = lax.all_gather(cache, "dp", axis=0, tiled=True).reshape(-1, feat)
-    lanes = width // n_expert
-    piece = lax.all_to_all(
-        proj_weight.reshape(-1, n_expert, lanes), "expert", split_axis=1, concat_axis=0, tiled=True
-    ).reshape(feat, lanes)
-    part = dot(feats, piece).astype(BF)
-    projected = lax.all_gather(part, ("dp", "expert"), axis=1, tiled=True)
-    values = projected.astype(F32)
-    mean_square = jnp.mean(values * values, axis=1)
-    table = (values * lax.rsqrt(mean_square + 1e-06)[:, None] * norm_gain[None, :]).astype(BF)
-    table_rows = table.shape[0]
+    block = cache.shape[1]
+
+    n_dp = lax.axis_size("dp")
+    model_width = norm_gain.shape[0]
 
     token_row = (
         requests.reshape(-1)[:, None] * block + jnp.arange(block, dtype=jnp.int32)[None, :]
@@ -59,15 +296,31 @@
     sent = dot(pick, scaled_grad).astype(BF).reshape(experts, capacity, width)
     grad_rows = lax.all_to_all(sent, "expert", split_axis=0, concat_axis=0, tiled=True)
     grad_rows = grad_rows.reshape(-1, width)
-    rows = lax.all_to_all(
-        slot_row.reshape(experts, capacity), "expert", split_axis=0, concat_axis=0, tiled=True
-    ).reshape(-1)
+
+    depth = proj_weight.shape[0]
+    padded = -(-depth // 16) * 16
+    groups = n_expert // n_dp
+    lanes = width // groups
+    feats = jnp.pad(
+        cache.reshape(-1, n_expert, depth), ((0, 0), (0, 0), (0, padded - depth))
+    ).reshape(-1, n_expert * padded)
+    proj = jnp.pad(proj_weight, ((0, padded - depth), (0, 0)))
+    proj = proj.reshape(padded, groups, lanes).transpose(1, 0, 2)
+    ids = jnp.pad(slot_row.reshape(experts, 1, capacity), ((0, 0), (0, 7), (0, 128 - capacity)))
+    blocks, got = make_table(n_dp, n_expert, feats, proj, ids)
+    projected = blocks.transpose(1, 2, 0, 3).reshape(-1, model_width)
+    values = projected.astype(F32)
+    mean_square = jnp.mean(values * values, axis=1)
+    table = (values * lax.rsqrt(mean_square + 1e-06)[:, None] * norm_gain[None, :]).astype(BF)
+    table_rows = table.shape[0]
+    rows = got[:, 0, :capacity].reshape(-1)
     select = (rows[:, None] == jnp.arange(table_rows, dtype=jnp.int32)[None, :]).astype(BF)
 
     gate_act = dot(table, gate_weight[0])
     up_act = dot(table, up_weight[0])
     half = (jax.nn.silu(gate_act) * up_act).astype(BF)
-    hidden = lax.all_gather(half, "dp", axis=1, tiled=True)
+    halves = share(n_dp, half)
+    hidden = halves.transpose(1, 0, 2).reshape(table_rows, -1)
     out_rows = dot(hidden, down_weight[0]).astype(BF)
     sent_out = dot(select, out_rows).astype(BF).reshape(-1, capacity, width)
     hidden_rows = dot(select, hidden).astype(BF)

time: 145 us -> 114 us (0.79)
  Pallas kernels: 0 us -> 52.5 us
  waiting for transfers between devices: 54.1 us -> 13.7 us
  blocking collectives: 19.7 us -> 0 us
  between operations: 14.2 us -> 0.84 us
  starting transfers between devices: 25.3 us -> 13.5 us
  local copies, waits for them, and re-layouts: 11.7 us -> 17.4 us
  matrix products: 16 us -> 11.8 us
    pallas_call x0 -> x2, Pallas kernels: none -> 52.5 us  [the longest x1 41.9 us: make_table(): pl.pallas_call(functools.partial(table_kernel, n_dp, n_expert), out_shape...]
    all_gather x1 -> x0, waiting for transfers between devices: 38.1 us -> none  [body(): projected = lax.all_gather(part, ('dp', 'expert'), axis=1, tiled=True)]
    all_gather x2 -> x0, blocking collectives: 19.7 us -> none  [the longest x1 10.6 us: body(): hidden = lax.all_gather(half, 'dp', axis=1, tiled=True)]
    all_to_all x2 -> x0, starting transfers between devices: 13.4 us -> none  [the longest x1 6.85 us: body(): lax.all_to_all(slot_row.reshape(experts, capacity), 'expert', split_axis=...]
    dot_general x7 -> x6, matrix products: 16 us -> 11.8 us  [dot(): return lax.dot_general(a, b, (dims, ((), ())), preferred_element_type=F32)]
    unnamed x14 -> x19, local copies, waits for them, and re-layouts: 0.04 us -> 3.39 us
    pad x0 -> x2, local copies, waits for them, and re-layouts: none -> 2.43 us  [the longest x1 1.72 us: body(): jnp.pad(cache.reshape(-1, n_expert, depth), ((0, 0), (0, 0), (0, padded -...]
    all_to_all x2 -> x0, local copies, waits for them, and re-layouts: 2.41 us -> none  [the longest x1 1.83 us: body(): lax.all_to_all(proj_weight.reshape(-1, n_expert, lanes), 'expert', split_...]
  transfers between devices with their start and end apart: 5 -> 2, of which waited for: 3 -> 1; matrix products, arithmetic and copies ran while one was open for 14% -> 21% of each run, Pallas kernels for 0% -> 46%
where the time goes in v2:
time: 114 us
  Pallas kernels  52.5 us (46%)
  local copies, waits for them, and re-layouts  17.4 us (15%)
  waiting for transfers between devices  13.7 us (12%)
  starting transfers between devices  13.5 us (12%)
  matrix products  11.8 us (10%)
  other arithmetic  3.98 us (3%)
    pallas_call x1, Pallas kernels, make_table(): pl.pallas_call(functools.partial(table_kernel, n_dp, n_expert), out_shape...  41.9 us
    all_to_all x1, waiting for transfers between devices, body(): lax.all_to_all(sent_out, 'expert', split_axis=0, concat_axis=0, tiled=True)  13.7 us
    dot_general x6, matrix products, dot(): return lax.dot_general(a, b, (dims, ((), ())), preferred_element_type=F32)  11.8 us
    pallas_call x1, Pallas kernels, share(): pl.pallas_call(functools.partial(share_kernel, n_dp), out_shape=jax.Shape...  10.6 us
    all_to_all x1, starting transfers between devices, body(): lax.all_to_all(sent_out, 'expert', split_axis=0, concat_axis=0, tiled=True)  6.8 us
    all_to_all x1, starting transfers between devices, body(): lax.all_to_all(sent, 'expert', split_axis=0, concat_axis=0, tiled=True)  6.71 us
    unnamed x19, local copies, waits for them, and re-layouts  3.39 us
  transfers between devices with their start and end apart: 2, of which 1 were waited for; matrix products, arithmetic and copies ran while one was open for 21% of the time, Pallas kernels for 46%

profile of v2, /device:TPU:13, one launch (start us, length us, event | category | flops | bytes accessed | tf_op | source)
XLA Modules:
  0.0 113.8 jit_solution(10491881885831757126)
XLA Ops:
  0.6 1.0 convert_reduce_fusion
  2.9 1.5 %convolution_convert_fusion.2 = bf16[320,1024]{1,0:T(8,128)(2,1)S(1)} fusion(bf16[256,1024]{1,0:T(8,128)(2,1)} %param.19, f32[256]{0:T(256)} %bitcast.54, s32[256]{0:T(256)S(1)} %multiply_add_fusion), kind=kOutput, calls=%fused_computation.15 | convolution fusion | flops 168968192 | bytes 1181696 | tf_op jit(solution)/shard_map/dot_general | solution.py:17
  4.4 1.0 reshape.114
  5.4 6.7 %all-to-all-start.1 = ((bf16[16,20,1024]{2,1,0:T(8,128)(2,1)}), bf16[16,20,1024]{2,1,0:T(8,128)(2,1)}, u32[]{:S(2)}, u32[]{:S(2)}) async-start(bf16[16,20,1024]{2,1,0:T(8,128)(2,1)} %reshape.114), calls=%async_computation.1 | async-start | bytes 1572864 | tf_op jit(solution)/shard_map/all_to_all | solution.py:297
  13.1 0.8 select_reduce_fusion
  14.6 1.9 %reshape.108 = bf16[128,16,72]{2,1,0:T(8,128)(2,1)S(1)} reshape(bf16[2,64,1152]{2,1,0:T(8,128)(2,1)} %param.10) | data formatting | bytes 589824 | tf_op jit(solution)/shard_map/reshape | solution.py:305
  16.5 1.2 %copy.43 = bf16[128,16,72]{0,2,1:T(8,128)(2,1)} copy(bf16[128,16,72]{2,1,0:T(8,128)(2,1)S(1)} %reshape.108) | data formatting | bytes 589824
  17.6 1.7 %pad.12.clone = bf16[128,16,80]{0,2,1:T(8,128)(2,1)} pad(bf16[128,16,72]{0,2,1:T(8,128)(2,1)} %copy.43, bf16[]{:T(256)} %constant.6.clone.1), padding=0_0x0_0x0_8 | pad | bytes 622594 | tf_op jit(solution)/shard_map/jit(_pad)/pad | solution.py:304
  19.4 1.1 %copy.33.feat_ref = bf16[128,1280]{1,0:T(8,128)(2,1)S(1)} copy(bf16[128,1280]{0,1:T(8,128)(2,1)} %bitcast.46) | data formatting | bytes 655360 | tf_op jit(solution)/shard_map/reshape | solution.py:306
  21.3 41.9 %shard_map.113 = (bf16[16,2,128,128]{3,2,1,0:T(8,128)(2,1)S(1)}, s32[16,8,128]{2,1,0:T(8,128)S(1)}) custom-call(bf16[128,1280]{1,0:T(8,128)(2,1)S(1)} %copy.33.feat_ref, bf16[8,80,128]{2,1,0:T(8,128)(2,1)S(1)} %bitcast_bitcast_fusion.proj_ref, s32[16,8,128]{2,1,0:T(8,128)S(1)} %pad.14.rows_ref), custom_call_target="tpu_custom_call" | custom-call | tf_op jit(solution)/shard_map/pallas_call | solution.py:220
  64.6 1.0 fusion.5
  65.6 0.8 copy-done.8
  66.4 1.0 fusion.17.half_ref
  67.4 10.6 %shard_map.114 = bf16[2,256,704]{2,1,0:T(8,128)(2,1)S(1)} custom-call(bf16[256,704]{1,0:T(8,128)(2,1)S(1)} %fusion.17.half_ref), custom_call_target="tpu_custom_call" | custom-call | tf_op jit(solution)/shard_map/pallas_call | solution.py:248
  78.1 0.9 copy-done.1
  79.0 2.3 %copy.40 = bf16[256,2,704]{0,2,1:T(8,128)(2,1)} copy(bf16[256,2,704]{2,0,1:T(8,128)(2,1)} %bitcast.45) | data formatting | bytes 1441792 | tf_op jit(solution)/shard_map/transpose | solution.py:323
  81.4 2.3 %convolution_convert_fusion.3 = bf16[320,1024]{1,0:T(8,128)(2,1)S(1)} fusion(bf16[256,1408]{0,1:T(8,128)(2,1)} %bitcast.49, bf16[1,1408,1024]{2,1,0:T(8,128)(2,1)S(1)} %copy-done, s32[320]{0:T(512)S(1)} %eq.47), kind=kOutput, calls=%fused_computation.16 | convolution fusion | flops 906641408 | bytes 4261120 | tf_op jit(solution)/shard_map/dot_general | solution.py:17
  83.7 1.0 reshape.112
  84.7 6.8 %all-to-all-start = ((bf16[16,20,1024]{2,1,0:T(8,128)(2,1)}), bf16[16,20,1024]{2,1,0:T(8,128)(2,1)}, u32[]{:S(2)}, u32[]{:S(2)}) async-start(bf16[16,20,1024]{2,1,0:T(8,128)(2,1)} %reshape.112), calls=%async_computation | async-start | bytes 1572864 | tf_op jit(solution)/shard_map/all_to_all | solution.py:328
  91.5 1.2 %reshape.115 = bf16[320,1024]{1,0:T(8,128)(2,1)S(1)} reshape(bf16[16,20,1024]{2,1,0:T(8,128)(2,1)} %all-to-all-done.1) | data formatting | bytes 1310720 | tf_op jit(solution)/shard_map/reshape | solution.py:298
  92.8 4.7 %fusion = bf16[1,1408,1024]{2,1,0:T(8,128)(2,1)} fusion(bf16[320,1024]{1,0:T(8,128)(2,1)S(1)} %reshape.115, bf16[256,1408]{0,1:T(8,128)(2,1)} %bitcast.50, s32[320]{0:T(512)S(1)} %eq.47), kind=kOutput, calls=%fused_computation.1 | convolution fusion | flops 1155407872 | bytes 4261120 | tf_op jit(solution)/shard_map/dot_general | solution.py:17
  97.5 13.7 %all-to-all-done = bf16[16,20,1024]{2,1,0:T(8,128)(2,1)} async-done(((bf16[16,20,1024]{2,1,0:T(8,128)(2,1)}), bf16[16,20,1024]{2,1,0:T(8,128)(2,1)}, u32[]{:S(2)}, u32[]{:S(2)}) %all-to-all-start) | async-done | bytes 655392 | tf_op jit(solution)/shard_map/all_to_all | solution.py:328
  111.2 1.2 %reshape.113 = bf16[320,1024]{1,0:T(8,128)(2,1)S(1)} reshape(bf16[16,20,1024]{2,1,0:T(8,128)(2,1)} %all-to-all-done) | data formatting | bytes 1310720 | tf_op jit(solution)/shard_map/reshape | solution.py:329
  112.5 1.3 %fusion.13 = bf16[256,1024]{1,0:T(8,128)(2,1)} fusion(bf16[320,1024]{1,0:T(8,128)(2,1)S(1)} %reshape.113, f32[256]{0:T(256)S(1)} %bitcast.55, s32[256]{0:T(256)S(1)} %copy-done.4), kind=kOutput, calls=%fused_computation.18 | convolution fusion | flops 168378368 | bytes 1181696 | tf_op jit(solution)/shard_map/dot_general | solution.py:17
  (32 shorter events, 5.2 us)
Async XLA Ops:
  0.6 80.7 %copy-start = (bf16[1,1408,1024]{2,1,0:T(8,128)(2,1)S(1)}, bf16[1,1408,1024]{2,1,0:T(8,128)(2,1)}, u32[]{:S(2)}) copy-start(bf16[1,1408,1024]{2,1,0:T(8,128)(2,1)} %param.18) | copy-start | bytes 8650756
  2.4 0.5 copy-start.3
  5.4 15.1 %copy-start.2 = (bf16[72,1024]{1,0:T(8,128)(2,1)S(1)}, bf16[72,1024]{1,0:T(8,128)(2,1)}, u32[]{:S(2)}) copy-start(bf16[72,1024]{1,0:T(8,128)(2,1)} %param.14) | copy-start | bytes 442372
  5.4 79.3 %all-to-all-start.1 = ((bf16[16,20,1024]{2,1,0:T(8,128)(2,1)}), bf16[16,20,1024]{2,1,0:T(8,128)(2,1)}, u32[]{:S(2)}, u32[]{:S(2)}) async-start(bf16[16,20,1024]{2,1,0:T(8,128)(2,1)} %reshape.114), calls=%async_computation.1 | async-start | bytes 1572864 | tf_op jit(solution)/shard_map/all_to_all | solution.py:297
  17.6 45.8 %copy-start.5 = (f32[2048]{0:T(1024)S(1)}, f32[2048]{0:T(1024)}, u32[]{:S(2)}) copy-start(f32[2048]{0:T(1024)} %param.15) | copy-start | bytes 24580
  21.3 43.3 %copy-start.7 = (bf16[1,2048,704]{1,2,0:T(8,128)(2,1)S(1)}, bf16[1,2048,704]{1,2,0:T(8,128)(2,1)}, u32[]{:S(2)}) copy-start(bf16[1,2048,704]{1,2,0:T(8,128)(2,1)} %param.16) | copy-start | bytes 8650756
  64.6 1.8 %copy-start.8 = (bf16[1,2048,704]{1,2,0:T(8,128)(2,1)S(1)}, bf16[1,2048,704]{1,2,0:T(8,128)(2,1)}, u32[]{:S(2)}) copy-start(bf16[1,2048,704]{1,2,0:T(8,128)(2,1)} %param.17) | copy-start | bytes 8650756
  78.1 0.9 copy-start.1
  84.7 26.5 %all-to-all-start = ((bf16[16,20,1024]{2,1,0:T(8,128)(2,1)}), bf16[16,20,1024]{2,1,0:T(8,128)(2,1)}, u32[]{:S(2)}, u32[]{:S(2)}) async-start(bf16[16,20,1024]{2,1,0:T(8,128)(2,1)} %reshape.112), calls=%async_computation | async-start | bytes 1572864 | tf_op jit(solution)/shard_map/all_to_all | solution.py:328
  92.8 19.7 %copy-start.4 = (s32[256]{0:T(256)S(1)}, s32[256]{0:T(256)}, u32[]{:S(2)}) copy-start(s32[256]{0:T(256)} %copy-done.3) | copy-start | bytes 3076
  92.8 19.7 %copy-start.6 = (f32[256,1]{0,1:T(1,128)S(1)}, f32[256,1]{0,1:T(1,128)}, u32[]{:S(2)}) copy-start(f32[256,1]{0,1:T(1,128)} %param.13) | copy-start | bytes 3076

commit v3 on v2

--- a/solution.py
+++ b/solution.py
@@ -79,10 +79,17 @@
 
     mine = e // groups == y
 
+    lanes = held.shape[2]
+
+    def group_of(j):
+        if len(proj_ref.shape) == 3:
+            return proj_ref.at[j]
+        return proj_ref.at[:, pl.ds(pl.multiple_of(j * lanes, lanes), lanes)]
+
     def send_proj(dy, dj):
         j = (e + dj) % groups
         return remote(
-            proj_ref.at[j],
+            group_of(j),
             held.at[e],
             proj_send.at[dy * groups + dj],
             proj_recv.at[e],
@@ -98,7 +105,7 @@
 
     @pl.when(mine)
     def _():
-        held[e] = proj_ref[e % groups]
+        held[e] = group_of(e % groups)[...]
 
     got_ref[e] = rows_ref[e]
 
@@ -110,7 +117,7 @@
 
     def await_proj(i):
         s = (e + i) % n_expert
-        remote(proj_ref.at[0], held.at[s], proj_send.at[0], proj_recv.at[s], other).wait_recv()
+        remote(held.at[s], held.at[s], proj_send.at[0], proj_recv.at[s], other).wait_recv()
 
     pl.when(jnp.logical_not(mine))(lambda: await_proj(0))
     loop(1, n_expert, await_proj)
@@ -142,26 +149,38 @@
             (y, (a + d) % far * near + b),
         )
 
+    p, q = b // 2, b % 2
+
+    def at(d, x, core):
+        return (a + far - d) % far * near + x * 2 + core
+
     def to_near(d, c, block):
+        x, core = (1 - p, q) if c == 0 else (p, 1 - q)
         return remote(
             tab_ref.at[block],
             tab_ref.at[block],
             near_send.at[d, c],
             near_recv.at[d, c],
-            (y, a * near + (b + c) % near),
+            (y, a * near + x * 2 + core),
         )
 
     for d in range(1, far):
         to_far(d, e).start()
-    for d in range(far):
-        block = (a + far - d) % far * near + b
-        if d:
-            to_far(d, block).wait_recv()
-        for c in range(1, near):
-            to_near(d, c, block).start()
-    for d in range(far):
-        for c in range(1, near):
-            to_near(d, c, (a + far - d) % far * near + (b + near - c) % near).wait_recv()
+    for d in range(far + 1):
+        if d < far:
+            block = (a + far - d) % far * near + b
+            if d:
+                to_far(d, block).wait_recv()
+            if near == 4:
+                to_near(d, 0, block).start()
+                to_near(d, 1, block).start()
+        if d and near == 4:
+            to_near(d - 1, 0, at(d - 1, 1 - p, q)).wait_recv()
+            to_near(d - 1, 2, at(d - 1, 1 - p, q)).start()
+    if near == 4:
+        for d in range(far):
+            to_near(d, 1, at(d, p, 1 - q)).wait_recv()
+            to_near(d, 2, at(d, 1 - p, 1 - q)).wait_recv()
 
     def await_row(i):
         s = (e + n_expert - i) % n_expert
@@ -180,9 +199,11 @@
         over_dp(d, y).wait_send()
     for d in range(1, far):
         to_far(d, e).wait_send()
-    for d in range(far):
-        for c in range(1, near):
-            to_near(d, c, (a + far - d) % far * near + b).wait_send()
+    if near == 4:
+        for d in range(far):
+            to_near(d, 0, at(d, p, q)).wait_send()
+            to_near(d, 1, at(d, p, q)).wait_send()
+            to_near(d, 2, at(d, 1 - p, q)).wait_send()
 
 
 def share_kernel(n_dp, half_ref, out_ref, send_sem, recv_sem):
@@ -213,20 +234,20 @@
     return [pl.BlockSpec(memory_space=pltpu.VMEM)] * count
 
 
-def make_table(n_dp, n_expert, feats, proj, rows):
+def make_table(n_dp, n_expert, lanes, feats, proj, rows):
     dma = pltpu.SemaphoreType.DMA
     near = 4 if n_expert % 4 == 0 else 1
     far = n_expert // near
     return pl.pallas_call(
         functools.partial(table_kernel, n_dp, n_expert),
         out_shape=(
-            jax.ShapeDtypeStruct((n_expert, n_dp, feats.shape[0], proj.shape[2]), BF),
+            jax.ShapeDtypeStruct((n_expert, n_dp, feats.shape[0], lanes), BF),
             jax.ShapeDtypeStruct(rows.shape, rows.dtype),
         ),
         in_specs=in_vmem(3),
         out_specs=tuple(in_vmem(2)),
         scratch_shapes=[
-            pltpu.VMEM((n_expert,) + proj.shape[1:], BF),
+            pltpu.VMEM((n_expert, proj.shape[-2], lanes), BF),
             dma((n_expert,)),
             dma((n_expert,)),
             dma((n_expert,)),
@@ -294,20 +315,23 @@
     token_weight = combine_weight[:, 0]
     scaled_grad = (token_weight[:, None] * cotangent.astype(F32)).astype(BF)
     sent = dot(pick, scaled_grad).astype(BF).reshape(experts, capacity, width)
-    grad_rows = lax.all_to_all(sent, "expert", split_axis=0, concat_axis=0, tiled=True)
-    grad_rows = grad_rows.reshape(-1, width)
-
     depth = proj_weight.shape[0]
     padded = -(-depth // 16) * 16
     groups = n_expert // n_dp
     lanes = width // groups
-    feats = jnp.pad(
-        cache.reshape(-1, n_expert, depth), ((0, 0), (0, 0), (0, padded - depth))
-    ).reshape(-1, n_expert * padded)
+    spot = jnp.arange(n_expert * padded, dtype=jnp.int32)
+    origin = jnp.where(spot % padded < depth, spot // padded * depth + spot % padded, -1)
+    source = jnp.arange(n_expert * depth, dtype=jnp.int32)
+    spread = (source[:, None] == origin[None, :]).astype(BF)
+    feats = dot(cache.reshape(-1, n_expert * depth), spread).astype(BF)
     proj = jnp.pad(proj_weight, ((0, padded - depth), (0, 0)))
-    proj = proj.reshape(padded, groups, lanes).transpose(1, 0, 2)
+    if lanes % 128:
+        proj = proj.reshape(padded, groups, lanes).transpose(1, 0, 2)
     ids = jnp.pad(slot_row.reshape(experts, 1, capacity), ((0, 0), (0, 7), (0, 128 - capacity)))
-    blocks, got = make_table(n_dp, n_expert, feats, proj, ids)
+    blocks, got = make_table(n_dp, n_expert, lanes, feats, proj, ids)
+    sent, got = lax.optimization_barrier((sent, got))
+    grad_rows = lax.all_to_all(sent, "expert", split_axis=0, concat_axis=0, tiled=True)
+    grad_rows = grad_rows.reshape(-1, width)
     projected = blocks.transpose(1, 2, 0, 3).reshape(-1, model_width)
     values = projected.astype(F32)
     mean_square = jnp.mean(values * values, axis=1)
@@ -320,11 +344,14 @@
     up_act = dot(table, up_weight[0])
     half = (jax.nn.silu(gate_act) * up_act).astype(BF)
     halves = share(n_dp, half)
-    hidden = halves.transpose(1, 0, 2).reshape(table_rows, -1)
-    out_rows = dot(hidden, down_weight[0]).astype(BF)
+    down = down_weight[0].reshape(n_dp, half.shape[1], width)
+    out_rows = dot(halves, down, ((0, 2), (0, 1))).astype(BF)
     sent_out = dot(select, out_rows).astype(BF).reshape(-1, capacity, width)
-    hidden_rows = dot(select, hidden).astype(BF)
-    down_grad = dot(hidden_rows, grad_rows, ((0,), (0,))).astype(BF)
+    down_grad = [
+        dot(dot(select, halves[i]).astype(BF), grad_rows, ((0,), (0,))).astype(BF)
+        for i in range(n_dp)
+    ]
+    down_grad = jnp.concatenate(down_grad, axis=0)
     returned = lax.all_to_all(sent_out, "expert", split_axis=0, concat_axis=0, tiled=True)
     token_out = dot(pick, returned.reshape(experts * capacity, width), ((0,), (0,)))
     mixed = (token_weight[:, None] * token_out).astype(BF)

time: 114 us -> 112 us (0.982)
  local copies, waits for them, and re-layouts: 17.4 us -> 9.37 us
  matrix products: 11.8 us -> 18.3 us
  other arithmetic: 3.98 us -> 10.2 us
  Pallas kernels: 52.5 us -> 47 us
  waiting for transfers between devices: 13.7 us -> 11.8 us
    dot_general x6 -> x8, matrix products: 11.8 us -> 18.3 us  [dot(): return lax.dot_general(a, b, (dims, ((), ())), preferred_element_type=F32)]
    pallas_call x1, Pallas kernels: 41.9 us -> 36.6 us  [make_table(): pl.pallas_call(functools.partial(table_kernel, n_dp, n_expert), out_shape...]
    broadcast_in_dim x0 -> x1, other arithmetic: none -> 3.64 us  [body(): return (mixed, down_grad[None])]
    reshape x2 -> x0, local copies, waits for them, and re-layouts: 3.04 us -> none  [the longest x1 1.9 us: body(): cache.reshape(-1, n_expert, depth)]
    transpose x2 -> x0, local copies, waits for them, and re-layouts: 2.3 us -> none  [the longest x1 2.27 us: body(): hidden = halves.transpose(1, 0, 2).reshape(table_rows, -1)]
    all_to_all x1, waiting for transfers between devices: 13.7 us -> 11.8 us  [body(): lax.all_to_all(sent_out, 'expert', split_axis=0, concat_axis=0, tiled=True)]
    unnamed x19 -> x14, local copies, waits for them, and re-layouts: 3.39 us -> 1.87 us
    reduce_sum x1, other arithmetic: 0.29 us -> 1.51 us  [body(): mean_square = jnp.mean(values * values, axis=1)]
  transfers between devices with their start and end apart: 2 -> 2, of which waited for: 1 -> 1; matrix products, arithmetic and copies ran while one was open for 21% -> 18% of each run, Pallas kernels for 46% -> 9%
where the time goes in v3:
time: 112 us; the launch traced here: 111 us
  Pallas kernels  47 us (42%)
  matrix products  18.3 us (16%)
  starting transfers between devices  13.9 us (12%)
  waiting for transfers between devices  11.8 us (11%)
  other arithmetic  10.2 us (9%)
  local copies, waits for them, and re-layouts  9.37 us (8%)
    pallas_call x1, Pallas kernels, make_table(): pl.pallas_call(functools.partial(table_kernel, n_dp, n_expert), out_shape...  36.6 us
    dot_general x8, matrix products, dot(): return lax.dot_general(a, b, (dims, ((), ())), preferred_element_type=F32)  18.3 us
    all_to_all x1, waiting for transfers between devices, body(): lax.all_to_all(sent_out, 'expert', split_axis=0, concat_axis=0, tiled=True)  11.8 us
    pallas_call x1, Pallas kernels, share(): pl.pallas_call(functools.partial(share_kernel, n_dp), out_shape=jax.Shape...  10.4 us
    all_to_all x1, starting transfers between devices, body(): lax.all_to_all(sent, 'expert', split_axis=0, concat_axis=0, tiled=True)  6.96 us
    all_to_all x1, starting transfers between devices, body(): lax.all_to_all(sent_out, 'expert', split_axis=0, concat_axis=0, tiled=True)  6.92 us
    broadcast_in_dim x1, other arithmetic, body(): return (mixed, down_grad[None])  3.64 us
  transfers between devices with their start and end apart: 2, of which 1 were waited for; matrix products, arithmetic and copies ran while one was open for 18% of the time, Pallas kernels for 9%

profile of v3, /device:TPU:13, one launch (start us, length us, event | category | flops | bytes accessed | tf_op | source)
XLA Modules:
  0.0 111.4 jit_solution(1968324025464937705)
XLA Ops:
  1.3 0.9 multiply_reduce_fusion
  2.3 0.9 convert_reduce_fusion
  4.3 1.5 %convolution_convert_fusion.3 = bf16[320,1024]{1,0:T(8,128)(2,1)S(1)} fusion(bf16[256,1024]{1,0:T(8,128)(2,1)} %param.19, f32[256]{0:T(256)} %bitcast.54, s32[256]{0:T(256)S(1)} %multiply_add_fusion), kind=kOutput, calls=%fused_computation.20 | convolution fusion | flops 168968192 | bytes 1181696 | tf_op jit(solution)/shard_map/dot_general | solution.py:17
  5.8 1.0 reshape.120
  7.8 2.2 %fusion.7.feat_ref = bf16[128,1280]{1,0:T(8,128)(2,1)S(1)} fusion(bf16[128,1152]{1,0:T(8,128)(2,1)} %bitcast.56, s32[1280]{0:T(1024)} %fusion.49), kind=kOutput, calls=%fused_computation.11 | convolution fusion | flops 379125760 | bytes 627712 | tf_op jit(solution)/shard_map/dot_general | solution.py:17
  10.1 36.6 %shard_map.113 = (bf16[16,2,128,128]{3,2,1,0:T(8,128)(2,1)S(1)}, s32[16,8,128]{2,1,0:T(8,128)S(1)}) custom-call(bf16[128,1280]{1,0:T(8,128)(2,1)S(1)} %fusion.7.feat_ref, bf16[80,1024]{1,0:T(8,128)(2,1)S(1)} %pad.8.proj_ref, s32[16,8,128]{2,1,0:T(8,128)S(1)} %pad.9.rows_ref), custom_call_target="tpu_custom_call" | custom-call | tf_op jit(solution)/shard_map/pallas_call | solution.py:241
  46.7 1.0 copy-done.1
  47.7 7.0 %all-to-all-start.1 = ((bf16[16,20,1024]{2,1,0:T(8,128)(2,1)}), bf16[16,20,1024]{2,1,0:T(8,128)(2,1)}, u32[]{:S(2)}, u32[]{:S(2)}) async-start(bf16[16,20,1024]{2,1,0:T(8,128)(2,1)} %reshape.120), calls=%async_computation.1 | async-start | bytes 1572864 | tf_op jit(solution)/shard_map/all_to_all | solution.py:333
  54.6 1.5 %fusion.8 = f32[2,128]{1,0:T(2,128)S(1)} fusion(bf16[16,2,128,128]{3,2,1,0:T(8,128)(2,1)} %copy-done.1), kind=kLoop, calls=%fused_computation.12 | loop fusion | flops 1572608 | bytes 1049600 | tf_op jit(solution)/shard_map/reduce_sum | solution.py:337
  56.2 1.6 %fusion.19 = bf16[2,128,16,128]{3,1,0,2:T(8,128)(2,1)S(1)} fusion(bf16[16,2,128,128]{3,2,1,0:T(8,128)(2,1)} %copy-done.1, f32[16,128]{1,0:T(8,128)S(1)} %bitcast.53, f32[2,128]{1,0:T(2,128)S(1)} %add_rsqrt_fusion), kind=kLoop, calls=%fused_computation.27 | loop fusion | flops 2097152 | bytes 2106368 | tf_op jit(solution)/shard_map/convert_element_type | solution.py:338
  57.8 1.6 %copy.28 = bf16[2,128,16,128]{3,2,1,0:T(8,128)(2,1)} copy(bf16[2,128,16,128]{3,1,0,2:T(8,128)(2,1)S(1)} %fusion.19) | data formatting | bytes 2097152 | tf_op jit(solution)/shard_map/convert_element_type | solution.py:338
  59.6 3.3 %fusion.4 = f32[256,704]{1,0:T(8,128)S(1)} fusion(bf16[1,2048,704]{1,2,0:T(8,128)(2,1)} %param.16, bf16[32,8,16,128]{3,2,1,0:T(8,128)(2,1)} %bitcast.49), kind=kOutput, calls=%fused_computation.6 | convolution fusion | flops 738197504 | bytes 4653056 | tf_op jit(solution)/shard_map/dot_general | solution.py:17
  62.9 1.0 fusion.16.half_ref
  64.0 10.4 %shard_map.114 = bf16[2,256,704]{2,1,0:T(8,128)(2,1)S(1)} custom-call(bf16[256,704]{1,0:T(8,128)(2,1)S(1)} %fusion.16.half_ref), custom_call_target="tpu_custom_call" | custom-call | tf_op jit(solution)/shard_map/pallas_call | solution.py:269
  75.3 2.3 %convolution_convert_fusion.2 = bf16[320,1024]{1,0:T(8,128)(2,1)S(1)} fusion(bf16[2,256,704]{2,1,0:T(8,128)(2,1)} %copy-done.2, bf16[2,704,1024]{2,1,0:T(8,128)(2,1)S(1)} %bitcast.48, s32[320]{0:T(512)S(1)} %eq.66), kind=kOutput, calls=%fused_computation.19 | convolution fusion | flops 906641408 | bytes 4261120 | tf_op jit(solution)/shard_map/dot_general | solution.py:17
  77.6 1.0 reshape.122
  78.6 6.9 %all-to-all-start = ((bf16[16,20,1024]{2,1,0:T(8,128)(2,1)}), bf16[16,20,1024]{2,1,0:T(8,128)(2,1)}, u32[]{:S(2)}, u32[]{:S(2)}) async-start(bf16[16,20,1024]{2,1,0:T(8,128)(2,1)} %reshape.122), calls=%async_computation | async-start | bytes 1572864 | tf_op jit(solution)/shard_map/all_to_all | solution.py:355
  85.6 1.2 %reshape.124 = bf16[320,1024]{1,0:T(8,128)(2,1)S(1)} reshape(bf16[16,20,1024]{2,1,0:T(8,128)(2,1)} %all-to-all-done.1) | data formatting | bytes 1310720 | tf_op jit(solution)/shard_map/reshape | solution.py:334
  86.8 3.3 %convolution_convert_fusion = bf16[704,1024]{1,0:T(8,128)(2,1)} fusion(bf16[320,1024]{1,0:T(8,128)(2,1)S(1)} %reshape.124, bf16[2,256,704]{2,1,0:T(8,128)(2,1)} %copy-done.2, s32[320]{0:T(512)S(1)} %eq.66), kind=kOutput, calls=%fused_computation.15 | convolution fusion | flops 577744896 | bytes 2491648 | tf_op jit(solution)/shard_map/dot_general | solution.py:17
  90.1 3.3 %convolution_convert_fusion.1 = bf16[704,1024]{1,0:T(8,128)(2,1)} fusion(bf16[320,1024]{1,0:T(8,128)(2,1)S(1)} %reshape.124, bf16[2,256,704]{2,1,0:T(8,128)(2,1)} %copy-done.2, s32[320]{0:T(512)S(1)} %eq.66), kind=kOutput, calls=%fused_computation.16 | convolution fusion | flops 577744896 | bytes 2491648 | tf_op jit(solution)/shard_map/dot_general | solution.py:17
  93.4 11.8 %all-to-all-done = bf16[16,20,1024]{2,1,0:T(8,128)(2,1)} async-done(((bf16[16,20,1024]{2,1,0:T(8,128)(2,1)}), bf16[16,20,1024]{2,1,0:T(8,128)(2,1)}, u32[]{:S(2)}, u32[]{:S(2)}) %all-to-all-start) | async-done | bytes 655392 | tf_op jit(solution)/shard_map/all_to_all | solution.py:355
  105.2 1.2 %reshape.123 = bf16[320,1024]{1,0:T(8,128)(2,1)S(1)} reshape(bf16[16,20,1024]{2,1,0:T(8,128)(2,1)} %all-to-all-done) | data formatting | bytes 1310720 | tf_op jit(solution)/shard_map/reshape | solution.py:356
  106.5 1.3 %fusion.12 = bf16[256,1024]{1,0:T(8,128)(2,1)} fusion(bf16[320,1024]{1,0:T(8,128)(2,1)S(1)} %reshape.123, f32[256]{0:T(256)S(1)} %bitcast.55, s32[256]{0:T(256)S(1)} %multiply_add_fusion), kind=kOutput, calls=%fused_computation.22 | convolution fusion | flops 168378368 | bytes 1181696 | tf_op jit(solution)/shard_map/dot_general | solution.py:17
  107.8 3.6 %maximum_bitcast_fusion = bf16[1,1408,1024]{2,1,0:T(8,128)(2,1)} fusion(bf16[704,1024]{1,0:T(8,128)(2,1)} %convolution_convert_fusion, bf16[704,1024]{1,0:T(8,128)(2,1)} %convolution_convert_fusion.1), kind=kLoop, calls=%fused_computation.3 | loop fusion | flops 5767168 | bytes 5767168 | tf_op jit(solution)/shard_map/broadcast_in_dim | solution.py:358
  (27 shorter events, 3.8 us)
Async XLA Ops:
  0.6 74.7 %copy-start = (bf16[1,1408,1024]{2,1,0:T(8,128)(2,1)S(1)}, bf16[1,1408,1024]{2,1,0:T(8,128)(2,1)}, u32[]{:S(2)}) copy-start(bf16[1,1408,1024]{2,1,0:T(8,128)(2,1)} %param.18) | copy-start | bytes 8650756
  7.8 48.4 %copy-start.4 = (f32[2048]{0:T(1024)S(1)}, f32[2048]{0:T(1024)}, u32[]{:S(2)}) copy-start(f32[2048]{0:T(1024)} %param.15) | copy-start | bytes 24580
  46.7 1.0 copy-start.1
  47.7 31.0 %all-to-all-start.1 = ((bf16[16,20,1024]{2,1,0:T(8,128)(2,1)}), bf16[16,20,1024]{2,1,0:T(8,128)(2,1)}, u32[]{:S(2)}, u32[]{:S(2)}) async-start(bf16[16,20,1024]{2,1,0:T(8,128)(2,1)} %reshape.120), calls=%async_computation.1 | async-start | bytes 1572864 | tf_op jit(solution)/shard_map/all_to_all | solution.py:333
  59.6 3.3 %copy-start.3 = (bf16[2,128,16,128]{3,2,1,0:T(8,128)(2,1)S(1)}, bf16[2,128,16,128]{3,2,1,0:T(8,128)(2,1)}, u32[]{:S(2)}) copy-start(bf16[2,128,16,128]{3,2,1,0:T(8,128)(2,1)} %copy.28) | copy-start | bytes 3145732
  59.6 3.3 %copy-start.6 = (bf16[1,2048,704]{1,2,0:T(8,128)(2,1)S(1)}, bf16[1,2048,704]{1,2,0:T(8,128)(2,1)}, u32[]{:S(2)}) copy-start(bf16[1,2048,704]{1,2,0:T(8,128)(2,1)} %param.17) | copy-start | bytes 8650756
  74.4 0.9 copy-start.2
  78.6 26.6 %all-to-all-start = ((bf16[16,20,1024]{2,1,0:T(8,128)(2,1)}), bf16[16,20,1024]{2,1,0:T(8,128)(2,1)}, u32[]{:S(2)}, u32[]{:S(2)}) async-start(bf16[16,20,1024]{2,1,0:T(8,128)(2,1)} %reshape.122), calls=%async_computation | async-start | bytes 1572864 | tf_op jit(solution)/shard_map/all_to_all | solution.py:355
  90.1 16.3 %copy-start.5 = (f32[256,1]{0,1:T(1,128)S(1)}, f32[256,1]{0,1:T(1,128)}, u32[]{:S(2)}) copy-start(f32[256,1]{0,1:T(1,128)} %param.13) | copy-start | bytes 3076

commit v4 on v3

--- a/solution.py
+++ b/solution.py
@@ -47,6 +47,7 @@
     held,
     proj_send,
     proj_recv,
+    pass_send,
     row_send,
     row_recv,
     dp_send,
@@ -86,41 +87,51 @@
             return proj_ref.at[j]
         return proj_ref.at[:, pl.ds(pl.multiple_of(j * lanes, lanes), lanes)]
 
-    def send_proj(dy, dj):
+    def send_proj(dj):
         j = (e + dj) % groups
         return remote(
-            group_of(j),
-            held.at[e],
-            proj_send.at[dy * groups + dj],
-            proj_recv.at[e],
-            ((y + dy) % n_dp, y * groups + j),
-        )
-
-    for dj in range(groups):
-        for dy in range(n_dp):
-            if dy == 0 and dj == 0:
-                pl.when(jnp.logical_not(mine))(lambda: send_proj(0, 0).start())
-            else:
-                send_proj(dy, dj).start()
+            group_of(j), held.at[e], proj_send.at[dj], proj_recv.at[e], (y, y * groups + j)
+        )
+
+    pl.when(jnp.logical_not(mine))(lambda: send_proj(0).start())
+    for dj in range(1, groups):
+        send_proj(dj).start()
+
+    got_ref[e] = rows_ref[e]
+
+    def send_row(i):
+        t = (e + i) % n_expert
+        return remote(rows_ref.at[t], got_ref.at[e], row_send.at[i], row_recv.at[i], (y, t))
+
+    loop(1, n_expert, lambda i: send_row(i).start())
+
+    def await_proj(i):
+        s = (e + n_expert - i) % n_expert
+        remote(held.at[s], held.at[s], proj_send.at[0], proj_recv.at[s], other).wait_recv()
+
+    def pass_on(i, d):
+        s = (e + n_expert - i) % n_expert
+        return remote(
+            held.at[s], held.at[s], pass_send.at[d, i], proj_recv.at[s], ((y + d) % n_dp, e)
+        )
 
     @pl.when(mine)
     def _():
         held[e] = group_of(e % groups)[...]
 
-    got_ref[e] = rows_ref[e]
-
-    def send_row(i):
-        t = (e + i) % n_expert
-        return remote(rows_ref.at[t], got_ref.at[e], row_send.at[i], row_recv.at[i], (y, t))
-
-    loop(1, n_expert, lambda i: send_row(i).start())
-
-    def await_proj(i):
-        s = (e + i) % n_expert
-        remote(held.at[s], held.at[s], proj_send.at[0], proj_recv.at[s], other).wait_recv()
-
-    pl.when(jnp.logical_not(mine))(lambda: await_proj(0))
-    loop(1, n_expert, await_proj)
+        def relay(i):
+            for d in range(1, n_dp):
+                pass_on(i, d).start()
+
+        relay(0)
+
+        def step(i):
+            await_proj(i)
+            relay(i)
+
+        loop(1, n_expert, step)
+
+    pl.when(jnp.logical_not(mine))(lambda: loop(0, n_expert, await_proj))
 
     weight = held[...].reshape(-1, held.shape[2])
     part = jnp.dot(feat_ref[...], weight, preferred_element_type=jnp.float32)
@@ -189,11 +200,18 @@
         ).wait_recv()
 
     loop(1, n_expert, await_row)
-    pl.when(jnp.logical_not(mine))(lambda: send_proj(0, 0).wait_send())
-    for dj in range(groups):
-        for dy in range(n_dp):
-            if dy or dj:
-                send_proj(dy, dj).wait_send()
+    pl.when(jnp.logical_not(mine))(lambda: send_proj(0).wait_send())
+    for dj in range(1, groups):
+        send_proj(dj).wait_send()
+
+    @pl.when(mine)
+    def _():
+        def sent(i):
+            for d in range(1, n_dp):
+                pass_on(i, d).wait_send()
+
+        loop(0, n_expert, sent)
+
     loop(1, n_expert, lambda i: send_row(i).wait_send())
     for d in range(1, n_dp):
         over_dp(d, y).wait_send()
@@ -250,6 +268,7 @@
             pltpu.VMEM((n_expert, proj.shape[-2], lanes), BF),
             dma((n_expert,)),
             dma((n_expert,)),
+            dma((n_dp, n_expert)),
             dma((n_expert,)),
             dma((n_expert,)),
             dma((n_dp,)),
@@ -343,15 +362,14 @@
     gate_act = dot(table, gate_weight[0])
     up_act = dot(table, up_weight[0])
     half = (jax.nn.silu(gate_act) * up_act).astype(BF)
-    halves = share(n_dp, half)
+    halves, grad_rows = lax.optimization_barrier((share(n_dp, half), grad_rows))
     down = down_weight[0].reshape(n_dp, half.shape[1], width)
     out_rows = dot(halves, down, ((0, 2), (0, 1))).astype(BF)
     sent_out = dot(select, out_rows).astype(BF).reshape(-1, capacity, width)
-    down_grad = [
-        dot(dot(select, halves[i]).astype(BF), grad_rows, ((0,), (0,))).astype(BF)
-        for i in range(n_dp)
-    ]
-    down_grad = jnp.concatenate(down_grad, axis=0)
+    hidden_rows = jnp.concatenate(
+        [dot(select, halves[i]).astype(BF) for i in range(n_dp)], axis=1
+    )
+    down_grad = dot(hidden_rows, grad_rows, ((0,), (0,))).astype(BF)
     returned = lax.all_to_all(sent_out, "expert", split_axis=0, concat_axis=0, tiled=True)
     token_out = dot(pick, returned.reshape(experts * capacity, width), ((0,), (0,)))
     mixed = (token_weight[:, None] * token_out).astype(BF)

time: 112 us -> 110 us (0.982)
  other arithmetic: 10.2 us -> 6.55 us
  Pallas kernels: 47 us -> 45 us
  waiting for transfers between devices: 11.8 us -> 13.6 us
    broadcast_in_dim x1 -> x0, other arithmetic: 3.64 us -> none  [body(): return (mixed, down_grad[None])]
    pallas_call x1, Pallas kernels: 36.6 us -> 34.6 us  [make_table(): pl.pallas_call(functools.partial(table_kernel, n_dp, n_expert), out_shape...]
    all_to_all x1, waiting for transfers between devices: 11.8 us -> 13.6 us  [body(): lax.all_to_all(sent_out, 'expert', split_axis=0, concat_axis=0, tiled=True)]
    dot_general x8 -> x9, matrix products: 18.3 us -> 18.6 us  [dot(): return lax.dot_general(a, b, (dims, ((), ())), preferred_element_type=F32)]
  transfers between devices with their start and end apart: 2 -> 2, of which waited for: 1 -> 1; matrix products, arithmetic and copies ran while one was open for 18% -> 14% of each run, Pallas kernels for 9% -> 10%
where the time goes in v4:
time: 110 us
  Pallas kernels  45 us (41%)
  matrix products  18.6 us (17%)
  starting transfers between devices  14.6 us (13%)
  waiting for transfers between devices  13.6 us (12%)
  local copies, waits for them, and re-layouts  10.4 us (9%)
  other arithmetic  6.55 us (6%)
    pallas_call x1, Pallas kernels, make_table(): pl.pallas_call(functools.partial(table_kernel, n_dp, n_expert), out_shape...  34.6 us
    dot_general x9, matrix products, dot(): return lax.dot_general(a, b, (dims, ((), ())), preferred_element_type=F32)  18.6 us
    all_to_all x1, waiting for transfers between devices, body(): lax.all_to_all(sent_out, 'expert', split_axis=0, concat_axis=0, tiled=True)  13.6 us
    pallas_call x1, Pallas kernels, share(): pl.pallas_call(functools.partial(share_kernel, n_dp), out_shape=jax.Shape...  10.4 us
    all_to_all x1, starting transfers between devices, body(): lax.all_to_all(sent, 'expert', split_axis=0, concat_axis=0, tiled=True)  7.69 us
    all_to_all x1, starting transfers between devices, body(): lax.all_to_all(sent_out, 'expert', split_axis=0, concat_axis=0, tiled=True)  6.89 us
  transfers between devices with their start and end apart: 2, of which 1 were waited for; matrix products, arithmetic and copies ran while one was open for 14% of the time, Pallas kernels for 10%

profile of v4, /device:TPU:13, one launch (start us, length us, event | category | flops | bytes accessed | tf_op | source)
XLA Modules:
  0.0 109.6 jit_solution(12149690086578639457)
XLA Ops:
  1.3 0.9 multiply_reduce_fusion
  2.3 0.9 convert_reduce_fusion
  4.3 1.5 %convolution_convert_fusion.2 = bf16[320,1024]{1,0:T(8,128)(2,1)S(1)} fusion(bf16[256,1024]{1,0:T(8,128)(2,1)} %param.19, f32[256]{0:T(256)} %bitcast.51, s32[256]{0:T(256)S(1)} %multiply_add_fusion), kind=kOutput, calls=%fused_computation.19 | convolution fusion | flops 168968192 | bytes 1181696 | tf_op jit(solution)/shard_map/dot_general | solution.py:17
  5.8 1.0 reshape.120
  7.8 2.2 %fusion.8.feat_ref = bf16[128,1280]{1,0:T(8,128)(2,1)S(1)} fusion(bf16[128,1152]{1,0:T(8,128)(2,1)} %bitcast.53, s32[1280]{0:T(1024)} %fusion.47), kind=kOutput, calls=%fused_computation.12 | convolution fusion | flops 379125760 | bytes 627712 | tf_op jit(solution)/shard_map/dot_general | solution.py:17
  10.1 34.6 %shard_map.113 = (bf16[16,2,128,128]{3,2,1,0:T(8,128)(2,1)S(1)}, s32[16,8,128]{2,1,0:T(8,128)S(1)}) custom-call(bf16[128,1280]{1,0:T(8,128)(2,1)S(1)} %fusion.8.feat_ref, bf16[80,1024]{1,0:T(8,128)(2,1)S(1)} %pad.8.proj_ref, s32[16,8,128]{2,1,0:T(8,128)S(1)} %pad.9.rows_ref), custom_call_target="tpu_custom_call" | custom-call | tf_op jit(solution)/shard_map/pallas_call | solution.py:259
  44.7 1.0 copy-done.1
  45.7 7.7 %all-to-all-start = ((bf16[16,20,1024]{2,1,0:T(8,128)(2,1)}), bf16[16,20,1024]{2,1,0:T(8,128)(2,1)}, u32[]{:S(2)}, u32[]{:S(2)}) async-start(bf16[16,20,1024]{2,1,0:T(8,128)(2,1)} %reshape.120), calls=%async_computation | async-start | bytes 1572864 | tf_op jit(solution)/shard_map/all_to_all | solution.py:352
  53.3 1.5 %fusion.9 = f32[2,128]{1,0:T(2,128)S(1)} fusion(bf16[16,2,128,128]{3,2,1,0:T(8,128)(2,1)} %copy-done.1), kind=kLoop, calls=%fused_computation.13 | loop fusion | flops 1572608 | bytes 1049600 | tf_op jit(solution)/shard_map/reduce_sum | solution.py:356
  54.9 1.6 %fusion.20 = bf16[2,128,16,128]{3,1,0,2:T(8,128)(2,1)S(1)} fusion(bf16[16,2,128,128]{3,2,1,0:T(8,128)(2,1)} %copy-done.1, f32[16,128]{1,0:T(8,128)S(1)} %bitcast.50, f32[2,128]{1,0:T(2,128)S(1)} %add_rsqrt_fusion), kind=kLoop, calls=%fused_computation.26 | loop fusion | flops 2097152 | bytes 2106368 | tf_op jit(solution)/shard_map/convert_element_type | solution.py:357
  56.5 1.6 %copy.28 = bf16[2,128,16,128]{3,2,1,0:T(8,128)(2,1)} copy(bf16[2,128,16,128]{3,1,0,2:T(8,128)(2,1)S(1)} %fusion.20) | data formatting | bytes 2097152 | tf_op jit(solution)/shard_map/convert_element_type | solution.py:357
  58.3 3.3 %fusion.5 = f32[256,704]{1,0:T(8,128)S(1)} fusion(bf16[1,2048,704]{1,2,0:T(8,128)(2,1)} %param.16, bf16[32,8,16,128]{3,2,1,0:T(8,128)(2,1)} %bitcast.46), kind=kOutput, calls=%fused_computation.7 | convolution fusion | flops 738197504 | bytes 4653056 | tf_op jit(solution)/shard_map/dot_general | solution.py:17
  61.6 1.1 fusion.17.half_ref
  62.7 10.4 %shard_map.114 = bf16[2,256,704]{2,1,0:T(8,128)(2,1)S(1)} custom-call(bf16[256,704]{1,0:T(8,128)(2,1)S(1)} %fusion.17.half_ref), custom_call_target="tpu_custom_call" | custom-call | tf_op jit(solution)/shard_map/pallas_call | solution.py:288
  74.0 1.2 %reshape.122 = bf16[320,1024]{1,0:T(8,128)(2,1)S(1)} reshape(bf16[16,20,1024]{2,1,0:T(8,128)(2,1)} %all-to-all-done) | data formatting | bytes 1310720 | tf_op jit(solution)/shard_map/reshape | solution.py:353
  75.3 3.2 %convolution_convert_fusion.1 = bf16[320,1024]{1,0:T(8,128)(2,1)} fusion(bf16[2,256,704]{2,1,0:T(8,128)(2,1)} %copy-done.2, bf16[2,704,1024]{2,1,0:T(8,128)(2,1)S(1)} %bitcast.45, s32[320]{0:T(512)S(1)} %eq.66), kind=kOutput, calls=%fused_computation.18 | convolution fusion | flops 906641408 | bytes 4261120 | tf_op jit(solution)/shard_map/dot_general | solution.py:17
  78.5 2.0 %reshape.123 = bf16[16,20,1024]{2,1,0:T(8,128)(2,1)} reshape(bf16[320,1024]{1,0:T(8,128)(2,1)} %convolution_convert_fusion.1) | data formatting | bytes 1310720 | tf_op jit(solution)/shard_map/reshape | solution.py:368
  80.5 6.9 %all-to-all-start.1 = ((bf16[16,20,1024]{2,1,0:T(8,128)(2,1)}), bf16[16,20,1024]{2,1,0:T(8,128)(2,1)}, u32[]{:S(2)}, u32[]{:S(2)}) async-start(bf16[16,20,1024]{2,1,0:T(8,128)(2,1)} %reshape.123), calls=%async_computation.1 | async-start | bytes 1572864 | tf_op jit(solution)/shard_map/all_to_all | solution.py:373
  87.4 1.3 %convolution_convert_fusion.3 = bf16[320,704]{1,0:T(8,128)(2,1)S(1)} fusion(bf16[2,256,704]{2,1,0:T(8,128)(2,1)} %copy-done.2, s32[320]{0:T(512)S(1)} %eq.66), kind=kOutput, calls=%fused_computation.23 | convolution fusion | flops 115650560 | bytes 845056 | tf_op jit(solution)/shard_map/dot_general | solution.py:17
  88.7 1.3 %convolution_convert_fusion.4 = bf16[320,704]{1,0:T(8,128)(2,1)S(1)} fusion(bf16[2,256,704]{2,1,0:T(8,128)(2,1)} %copy-done.2, s32[320]{0:T(512)S(1)} %eq.66), kind=kOutput, calls=%fused_computation.24 | convolution fusion | flops 115650560 | bytes 845056 | tf_op jit(solution)/shard_map/dot_general | solution.py:17
  90.1 3.4 %fusion.1 = bf16[1,1408,1024]{2,1,0:T(8,128)(2,1)} fusion(bf16[320,1024]{1,0:T(8,128)(2,1)S(1)} %reshape.122, bf16[320,704]{1,0:T(8,128)(2,1)S(1)} %convolution_convert_fusion.3, bf16[320,704]{1,0:T(8,128)(2,1)S(1)} %convolution_convert_fusion.4), kind=kOutput, calls=%fused_computation.3 | convolution fusion | flops 925990912 | bytes 4440064 | tf_op jit(solution)/shard_map/dot_general | solution.py:17
  93.5 13.6 %all-to-all-done.1 = bf16[16,20,1024]{2,1,0:T(8,128)(2,1)} async-done(((bf16[16,20,1024]{2,1,0:T(8,128)(2,1)}), bf16[16,20,1024]{2,1,0:T(8,128)(2,1)}, u32[]{:S(2)}, u32[]{:S(2)}) %all-to-all-start.1) | async-done | bytes 655392 | tf_op jit(solution)/shard_map/all_to_all | solution.py:373
  107.0 1.2 %reshape.124 = bf16[320,1024]{1,0:T(8,128)(2,1)S(1)} reshape(bf16[16,20,1024]{2,1,0:T(8,128)(2,1)} %all-to-all-done.1) | data formatting | bytes 1310720 | tf_op jit(solution)/shard_map/reshape | solution.py:374
  108.3 1.3 %fusion.13 = bf16[256,1024]{1,0:T(8,128)(2,1)} fusion(bf16[320,1024]{1,0:T(8,128)(2,1)S(1)} %reshape.124, f32[256]{0:T(256)S(1)} %bitcast.52, s32[256]{0:T(256)S(1)} %multiply_add_fusion), kind=kOutput, calls=%fused_computation.21 | convolution fusion | flops 168378368 | bytes 1181696 | tf_op jit(solution)/shard_map/dot_general | solution.py:17
  (27 shorter events, 3.8 us)
Async XLA Ops:
  0.6 74.6 %copy-start = (bf16[1,1408,1024]{2,1,0:T(8,128)(2,1)S(1)}, bf16[1,1408,1024]{2,1,0:T(8,128)(2,1)}, u32[]{:S(2)}) copy-start(bf16[1,1408,1024]{2,1,0:T(8,128)(2,1)} %param.18) | copy-start | bytes 8650756
  7.8 47.1 %copy-start.4 = (f32[2048]{0:T(1024)S(1)}, f32[2048]{0:T(1024)}, u32[]{:S(2)}) copy-start(f32[2048]{0:T(1024)} %param.15) | copy-start | bytes 24580
  44.7 1.0 copy-start.1
  45.7 28.4 %all-to-all-start = ((bf16[16,20,1024]{2,1,0:T(8,128)(2,1)}), bf16[16,20,1024]{2,1,0:T(8,128)(2,1)}, u32[]{:S(2)}, u32[]{:S(2)}) async-start(bf16[16,20,1024]{2,1,0:T(8,128)(2,1)} %reshape.120), calls=%async_computation | async-start | bytes 1572864 | tf_op jit(solution)/shard_map/all_to_all | solution.py:352
  58.3 3.3 %copy-start.3 = (bf16[2,128,16,128]{3,2,1,0:T(8,128)(2,1)S(1)}, bf16[2,128,16,128]{3,2,1,0:T(8,128)(2,1)}, u32[]{:S(2)}) copy-start(bf16[2,128,16,128]{3,2,1,0:T(8,128)(2,1)} %copy.28) | copy-start | bytes 3145732
  58.3 3.3 %copy-start.6 = (bf16[1,2048,704]{1,2,0:T(8,128)(2,1)S(1)}, bf16[1,2048,704]{1,2,0:T(8,128)(2,1)}, u32[]{:S(2)}) copy-start(bf16[1,2048,704]{1,2,0:T(8,128)(2,1)} %param.17) | copy-start | bytes 8650756
  73.1 0.9 copy-start.2
  80.5 26.6 %all-to-all-start.1 = ((bf16[16,20,1024]{2,1,0:T(8,128)(2,1)}), bf16[16,20,1024]{2,1,0:T(8,128)(2,1)}, u32[]{:S(2)}, u32[]{:S(2)}) async-start(bf16[16,20,1024]{2,1,0:T(8,128)(2,1)} %reshape.123), calls=%async_computation.1 | async-start | bytes 1572864 | tf_op jit(solution)/shard_map/all_to_all | solution.py:373
  90.0 18.2 %copy-start.5 = (f32[256,1]{0,1:T(1,128)S(1)}, f32[256,1]{0,1:T(1,128)}, u32[]{:S(2)}) copy-start(f32[256,1]{0,1:T(1,128)} %param.13) | copy-start | bytes 3076
